TPU v7x, 32 devices: a whole 2x2x4 slice. The times are simulated.
32 devices in a mesh: groups: 2 (over y), fsdp: 4 (over z), tp: 2 (over x), sub: 2 (over core).
Axes of the slice: x: 2, y: 2, z: 4, core: 2. Of those that a mesh axis runs over, the one named last changes fastest.
Arguments:
- hidden: bfloat16 [4, 1024, 14336], P(('groups', 'sub'), 'tp', 'fsdp'), parts along dimension 0, may hold values from -6 to 6
- cotangent: bfloat16 [4, 1024, 4096], P(('groups', 'sub'), 'fsdp', 'tp'), parts along dimension 0, may hold values from -6 to 6
- down_projection_weight: bfloat16 [14336, 4096], P('fsdp', 'tp'), may hold values from -0.046875 to 0.046875
- adapter_first_factor: bfloat16 [4, 14336, 64], P('fsdp'), may hold values from -0.046875 to 0.046875
- adapter_second_factor: bfloat16 [4, 64, 4096], P('fsdp', None, 'tp'), may hold values from -0.09375 to 0.09375
- shard_adapter_index: int32 [4, 4, 2], P(('groups', 'sub')), parts along dimension 0, may hold values from 0 to 3, as said below
- member: int32 [4, 1024, 2], P(('groups', 'sub')), parts along dimension 0, may hold values from 0 to 1, as said below
Outputs:
- hidden_grad: bfloat16 [4, 1024, 14336], P(('groups', 'sub'), 'tp', 'fsdp'), parts along dimension 0
- a_grad: float32 [8, 14336, 64], P(('groups', 'fsdp'), None, ('tp', 'sub')), parts along dimension 0
- b_grad: float32 [8, 64, 4096], P(('groups', 'fsdp'), None, ('tp', 'sub')), parts along dimension 0
There are 2 independent parts, one for each index of `groups`. A program takes and returns all parts, laid end to end along the dimension named above; an argument that names none is the same for every part. Nothing has to cross between parts.
Inputs may be any that keep to these rules, and one draw needn't show every extreme that they name: `shard_adapter_index`: the 2 adapters listed for one data shard have different owners (owner = id); some owner appears in every shard's list of the part. `member`: each row has exactly one 1; every slot of every shard's list has rows.
All inputs are finite; a program needn't handle non-finite values.
Results may differ from a plain program's by a relative error of at most 0.015.
Values may be sent and summed in bfloat16 or wider, within the bound.
A program may use at most 192 MiB of HBM per device.

v0:
```python
import jax
import jax.numpy as jnp
from jax import lax
from jax.sharding import PartitionSpec as P

adapter_scale = 2.0


def shards(
    hidden,
    cotangent,
    down_projection_weight,
    adapter_first_factor,
    adapter_second_factor,
    shard_adapter_index,
    member,
):
    fsdp_count = lax.axis_size("fsdp")
    fsdp_pos = lax.axis_index("fsdp")
    tp_pos = lax.axis_index("tp")
    shard_rows = cotangent.shape[1]
    rows_per_block = hidden.shape[1]
    shards_here = rows_per_block // shard_rows
    hidden_units_local = hidden.shape[2]
    rank_span = adapter_first_factor.shape[2]
    owned_adapter_count = adapter_first_factor.shape[0]
    adapter_total = owned_adapter_count * fsdp_count
    slot_count = shard_adapter_index.shape[2]
    slot_table = shard_adapter_index[0]
    row_marks = member[0]
    incoming_gradient = cotangent[0]
    shard_ids = lax.dynamic_index_in_dim(slot_table, fsdp_pos, 0, keepdims=False)
    shard_marks = lax.dynamic_slice_in_dim(row_marks, fsdp_pos * shard_rows, shard_rows, 0).astype(
        jnp.bfloat16
    )
    first_factor_pieces = lax.all_to_all(
        adapter_first_factor, "fsdp", split_axis=1, concat_axis=0, tiled=True
    )
    second_factors_gathered = lax.all_gather(adapter_second_factor, "fsdp", axis=0, tiled=True)
    b_factors = jnp.take(second_factors_gathered, shard_ids, axis=0)
    slot_adjoint = lax.dot_general(
        incoming_gradient,
        b_factors.reshape(slot_count * rank_span, -1),
        (((1,), (1,)), ((), ())),
        preferred_element_type=jnp.float32,
    )
    adjoint_local = jnp.sum(
        slot_adjoint.reshape(shard_rows, slot_count, rank_span)
        * shard_marks[:, :, None].astype(jnp.float32),
        axis=1,
    ).astype(jnp.bfloat16)
    rows_up, rows_low = lax.all_gather((cotangent, adjoint_local[None]), "fsdp", axis=1, tiled=True)
    base_rows = jnp.einsum(
        "bnd,fd->bnf", rows_up, down_projection_weight, preferred_element_type=jnp.float32
    )
    joined = jnp.concatenate([base_rows, rows_low.astype(jnp.float32)], axis=2)
    summed = lax.psum_scatter(
        joined.astype(jnp.bfloat16), "tp", scatter_dimension=1, tiled=True
    ).astype(jnp.float32)[0]
    frozen_portion = summed[:, :hidden_units_local]
    adjoint_rows = summed[:, hidden_units_local:].astype(jnp.bfloat16)
    block_ids = lax.dynamic_slice_in_dim(slot_table, tp_pos * shards_here, shards_here, 0)
    block_marks = (
        lax.dynamic_slice_in_dim(row_marks, tp_pos * rows_per_block, rows_per_block, 0)
        .astype(jnp.bfloat16)
        .reshape(shards_here, shard_rows, slot_count, 1)
    )
    selected_first = jnp.take(first_factor_pieces, block_ids.reshape(-1), axis=0).reshape(
        shards_here, slot_count, hidden_units_local, rank_span
    )
    adjoint_full_width = block_marks * adjoint_rows.reshape(shards_here, shard_rows, 1, rank_span)
    low_rank_contribution = jnp.einsum(
        "ptkr,pkfr->ptf", adjoint_full_width, selected_first, preferred_element_type=jnp.float32
    )
    hidden_gradient = (
        frozen_portion
        + adapter_scale * low_rank_contribution.reshape(rows_per_block, hidden_units_local)
    ).astype(jnp.bfloat16)[None]
    hidden_block = hidden[0].reshape(shards_here, shard_rows, hidden_units_local)
    latent_slots = jnp.einsum(
        "ptf,pkfr->ptkr", hidden_block, selected_first, preferred_element_type=jnp.float32
    )
    latent_part = jnp.sum(latent_slots * block_marks.astype(jnp.float32), axis=2).reshape(
        rows_per_block, rank_span
    )
    latent_rows = lax.psum(latent_part.astype(jnp.bfloat16), "fsdp")
    latent_every = lax.all_gather(latent_rows, "tp", axis=0, tiled=True)
    latent_own = lax.dynamic_slice_in_dim(latent_every, fsdp_pos * shard_rows, shard_rows, 0)
    slot_grads = jnp.einsum(
        "ptf,ptkr->pkfr", hidden_block, adjoint_full_width, preferred_element_type=jnp.float32
    )
    adapter_hits = (block_ids[:, :, None] == jnp.arange(adapter_total)[None, None, :]).astype(
        jnp.float32
    )
    first_factor_partial = adapter_scale * jnp.einsum(
        "pka,pkfr->afr", adapter_hits, slot_grads, precision=lax.Precision.HIGHEST
    )
    reduced = lax.psum_scatter(
        first_factor_partial.astype(jnp.bfloat16), ("tp", "sub"), scatter_dimension=2, tiled=True
    ).astype(jnp.float32)
    grad_a = lax.all_to_all(
        reduced.astype(jnp.bfloat16), "fsdp", split_axis=0, concat_axis=1, tiled=True
    ).astype(reduced.dtype)
    latent_full_width = (shard_marks[:, :, None] * latent_own[:, None, :]).reshape(
        shard_rows, slot_count * rank_span
    )
    slot_second_gradients = adapter_scale * lax.dot_general(
        latent_full_width,
        incoming_gradient,
        (((0,), (0,)), ((), ())),
        preferred_element_type=jnp.float32,
    ).reshape(slot_count, rank_span, -1)
    to_adapter = (shard_ids[:, None] == jnp.arange(adapter_total)[None, :]).astype(jnp.float32)
    spread = jnp.einsum(
        "ka,krd->ard", to_adapter, slot_second_gradients, precision=lax.Precision.HIGHEST
    )
    grad_rows = lax.psum_scatter(
        spread.astype(jnp.bfloat16), "fsdp", scatter_dimension=0, tiled=True
    )
    grad_b = lax.psum_scatter(grad_rows, "sub", scatter_dimension=2, tiled=True).astype(jnp.float32)
    return (hidden_gradient, grad_a, grad_b)


def solution(mesh):
    placed = (
        P(("groups", "sub"), "tp", "fsdp"),
        P(("groups", "sub"), "fsdp", "tp"),
        P("fsdp", "tp"),
        P("fsdp", None, None),
        P("fsdp", None, "tp"),
        P(("groups", "sub"), None, None),
        P(("groups", "sub"), None, None),
    )
    return jax.shard_map(
        shards,
        mesh=mesh,
        in_specs=placed,
        out_specs=(
            P(("groups", "sub"), "tp", "fsdp"),
            P(("groups", "fsdp"), None, ("tp", "sub")),
            P(("groups", "fsdp"), None, ("tp", "sub")),
        ),
        check_vma=False,
    )
```

profile of v0, /device:TPU:0, one launch (start us, length us, event | category | flops | bytes accessed | tf_op | source)
XLA Modules:
  0.0 521.0 jit_solution(1905588490081236786)
XLA Ops:
  7.2 15.3 %copy.74 = bf16[1,14336,64]{2,0,1:T(2,128)(2,1)} copy(bf16[1,14336,64]{1,2,0:T(8,128)(2,1)} %param.10) | data formatting | bytes 3670016 | tf_op args[3]
  22.4 0.5 broadcast.118
  22.9 79.7 %reduce.105 = bf16[14336,64]{1,0:T(8,128)(2,1)} reduce(bf16[14336,1,64]{2,1,0:T(2,128)(2,1)} %bitcast.190, bf16[]{:T(256)} %broadcast.118), dimensions={1}, to_apply=%bitcast.182.reduce_sub_computation | reduce | bytes 3670018
  102.7 5.5 %reshape.367 = bf16[4,2,114688]{2,1,0:T(2,128)(2,1)} reshape(bf16[14336,64]{1,0:T(8,128)(2,1)} %reduce.105) | data formatting | bytes 3670016
  108.2 6.3 %all-to-all-start = ((bf16[4,2,114688]{2,1,0:T(2,128)(2,1)}), bf16[4,2,114688]{2,1,0:T(2,128)(2,1)S(1)}, u32[]{:S(2)}, u32[]{:S(2)}) async-start(bf16[4,2,114688]{2,1,0:T(2,128)(2,1)} %reshape.367), calls=%async_computation.1 | async-start | bytes 3670016 | tf_op jit(solution)/shard_map/all_to_all | solution.py:36
  114.5 0.7 all-gather.6.cloned.1.call-update
  115.6 58.3 %all-to-all-done = bf16[4,2,114688]{2,1,0:T(2,128)(2,1)S(1)} async-done(((bf16[4,2,114688]{2,1,0:T(2,128)(2,1)}), bf16[4,2,114688]{2,1,0:T(2,128)(2,1)S(1)}, u32[]{:S(2)}, u32[]{:S(2)}) %all-to-all-start) | async-done | bytes 1835040 | tf_op jit(solution)/shard_map/all_to_all | solution.py:36
  173.9 4.4 reshape.368
  178.3 5.3 %copy.97 = bf16[1,14336,64]{2,1,0:T(8,128)(2,1)} copy(bf16[1,14336,64]{2,0,1:T(2,128)(2,1)} %bitcast.191) | data formatting | bytes 3670016
  183.7 4.5 copy.77
  188.2 2.2 gather_fusion.1
  190.4 3.5 fusion.9
  193.9 0.6 copy.198
  194.6 0.7 all-gather.4.cloned.1.call-update
  195.3 0.2 fusion.31
  195.6 1.8 gather_fusion
  197.5 0.5 fusion.11
  198.0 13.5 %all-gather = bf16[1024,64]{0,1:T(8,128)(2,1)S(1)} all-gather(bf16[256,64]{0,1:T(8,128)(2,1)S(1)} %multiply_reduce_fusion), channel_id=2, replica_groups=mesh['groups'=2,'fsdp'=4,'tp'=2,'sub'=2] {'fsdp'}, dimensions={0}, use_global_device_ids=true | all-gather | bytes 163840 | tf_op jit(solution)/shard_map/all_gather | solution.py:52
  211.6 0.2 copy.70
  211.7 16.1 %all-reduce.4.cloned.1.call-done = bf16[512,64]{0,1:T(8,128)(2,1)} async-done(((bf16[512,64]{0,1:T(8,128)(2,1)}), bf16[512,64]{0,1:T(8,128)(2,1)}) %all-reduce.4.cloned.1.call-update) | async-done | bytes 65552 | tf_op jit(solution)/shard_map/psum | solution.py:86
  227.8 5.3 %all_gather.15 = bf16[1024,64]{0,1:T(8,128)(2,1)S(1)} all-gather(bf16[512,64]{0,1:T(8,128)(2,1)} %all-reduce.4.cloned.1.call-done), channel_id=1, replica_groups=mesh['groups'=2,'fsdp'=4,'tp'=2,'sub'=2] {'tp'}, dimensions={0}, use_global_device_ids=true | all-gather | bytes 196608 | tf_op jit(solution)/shard_map/all_gather | solution.py:87
  233.2 0.3 convolution_multiply_fusion
  233.5 3.1 convolution_convert_fusion.1
  236.6 1.5 copy.85
  238.2 71.8 %all-gather.4.cloned.1.call-done = bf16[1,1024,2048]{2,1,0:T(8,128)(2,1)} async-done(((bf16[1,256,2048]{2,1,0:T(8,128)(2,1)}), bf16[1,1024,2048]{2,1,0:T(8,128)(2,1)}) %all-gather.4.cloned.1.call-update) | async-done | bytes 4194320 | tf_op jit(solution)/shard_map/all_gather | solution.py:52
  310.0 21.7 %fusion.1 = bf16[1,1024,3584]{2,1,0:T(8,128)(2,1)} fusion(bf16[3584,2048]{1,0:T(8,128)(2,1)} %param.9, bf16[1,1024,2048]{2,1,0:T(8,128)(2,1)} %all-gather.4.cloned.1.call-done), kind=kOutput, calls=%fused_computation.9 | convolution fusion | flops 15036055552 | bytes 26214400 | tf_op jit(solution)/shard_map/bnd,fd->bnf/dot_general | solution.py:53
  331.7 6.6 %pad_maximum_fusion = bf16[1,1024,3648]{2,1,0:T(8,128)(2,1)} fusion(bf16[1,1024,64]{2,1,0:T(8,128)(2,1)S(1)} %copy.70, bf16[1,1024,3584]{2,1,0:T(8,128)(2,1)} %fusion.1), kind=kLoop, calls=%fused_computation.4 | loop fusion | flops 14942208 | bytes 14942208 | tf_op jit(solution)/shard_map/concatenate | solution.py:56
  338.4 0.6 copy-done.4
  339.0 0.6 dynamic-slice.4
  340.3 48.2 %copy.94 = bf16[1,64,2048]{0,1,2:T(8,128)(2,1)} copy(bf16[1,64,2048]{2,1,0:T(8,128)(2,1)} %reduce-scatter.8.cloned.1.call-done) | data formatting | bytes 524288
  388.5 21.3 %bitcast_reduce_fusion = bf16[2048,64]{1,0:T(8,128)(2,1)} fusion(bf16[1,64,2048]{0,1,2:T(8,128)(2,1)} %copy.94), kind=kLoop, calls=%fused_computation.2 | loop fusion | bytes 524288
  409.7 0.3 all-reduce.6.cloned.1.call-start
  410.0 20.6 %reduce-scatter.6.cloned.1.call-done = bf16[1,512,3648]{2,1,0:T(8,128)(2,1)} async-done(((bf16[1,1024,3648]{2,1,0:T(8,128)(2,1)}), bf16[1,512,3648]{2,1,0:T(8,128)(2,1)}) %reduce-scatter.6.cloned.1.call-update) | async-done | bytes 3735568 | tf_op jit(solution)/shard_map/reduce_scatter | solution.py:57
  430.6 0.9 slice.18
  431.6 2.7 convolution_bitcast_fusion.1
  434.3 9.3 %fusion.3 = bf16[4,3584,64]{1,0,2:T(4,128)(2,1)} fusion(f32[2,2,3584,64]{2,3,1,0:T(8,128)S(1)} %convolution_bitcast_fusion.1, s32[2,2]{0,1:T(2,128)S(1)} %fusion.46), kind=kOutput, calls=%fused_computation.13 | convolution fusion | flops 45875216 | bytes 5505040 | tf_op jit(solution)/shard_map/pka,pkfr->afr/dot_general | solution.py:95
  443.7 14.2 %reshape_bitcast_fusion = bf16[1,64,1024]{0,1,2:T(8,128)(2,1)} fusion(bf16[1024,64]{1,0:T(8,128)(2,1)} %reduce-scatter.10.cloned.1.call-done), kind=kLoop, calls=%fused_computation.3 | loop fusion | bytes 262144
  457.9 17.4 %copy.95 = bf16[1,64,1024]{2,0,1:T(2,128)(2,1)S(1)} copy(bf16[1,64,1024]{0,1,2:T(8,128)(2,1)} %reshape_bitcast_fusion) | data formatting | bytes 262144
  475.3 0.8 copy.87
  476.0 4.1 bitcast_multiply_fusion
  480.2 12.5 %all-reduce.6.cloned.1.call-done = bf16[4,3584,64]{1,0,2:T(4,128)(2,1)} async-done(((bf16[4,3584,64]{1,0,2:T(4,128)(2,1)}), bf16[4,3584,64]{1,0,2:T(4,128)(2,1)}) %all-reduce.6.cloned.1.call-update) | async-done | bytes 1835024
  492.6 1.2 constant_dynamic-slice_fusion.3
  493.8 0.8 copy.80
  494.7 4.6 all-to-all-start.1
  499.3 7.0 %fusion = bf16[512,3584]{1,0:T(8,128)(2,1)} fusion(f32[2,256,3584]{2,1,0:T(8,128)} %bitcast_multiply_fusion, bf16[512,3648]{1,0:T(8,128)(2,1)} %bitcast.196), kind=kLoop, calls=%fused_computation.7 | loop fusion | flops 5505024 | bytes 14680064 | tf_op jit(solution)/shard_map/convert_element_type | solution.py:78
  506.3 6.0 %all-to-all-done.1 = bf16[4,3584,16]{1,2,0:T(8,128)(2,1)S(1)} async-done(((bf16[4,3584,16]{1,2,0:T(8,128)(2,1)}), bf16[4,3584,16]{1,2,0:T(8,128)(2,1)S(1)}, u32[]{:S(2)}, u32[]{:S(2)}) %all-to-all-start.1) | async-done | bytes 458784 | tf_op jit(solution)/shard_map/all_to_all | solution.py:101
  512.3 0.4 copy.81
  512.6 1.6 reshape.237
  (40 shorter events, 1.0 us)
Async XLA Ops:
  7.2 108.1 %copy-start = (s32[1,4,2]{1,2,0:T(2,128)S(1)}, s32[1,4,2]{1,2,0:T(2,128)}, u32[]{:S(2)}) copy-start(s32[1,4,2]{1,2,0:T(2,128)} %param.12) | copy-start | bytes 100
  102.7 12.8 %copy-start.3 = (s32[1,1024,2]{1,2,0:T(2,128)S(1)}, s32[1,1024,2]{1,2,0:T(2,128)}, u32[]{:S(2)}) copy-start(s32[1,1024,2]{1,2,0:T(2,128)} %param.13) | copy-start | bytes 24580
  108.2 65.8 %all-to-all-start = ((bf16[4,2,114688]{2,1,0:T(2,128)(2,1)}), bf16[4,2,114688]{2,1,0:T(2,128)(2,1)S(1)}, u32[]{:S(2)}, u32[]{:S(2)}) async-start(bf16[4,2,114688]{2,1,0:T(2,128)(2,1)} %reshape.367), calls=%async_computation.1 | async-start | bytes 3670016 | tf_op jit(solution)/shard_map/all_to_all | solution.py:36
  114.5 81.1 %all-gather.6.cloned.1.call-start = ((), (), s32[]{:S(2)}) async-start(), calls=%async_computation.6 | async-start | bytes 1310720 | tf_op jit(solution)/shard_map/all_gather | solution.py:39
  115.2 112.6 %all-reduce.4.cloned.1.call-start = ((), (), s32[]{:S(2)}) async-start(), calls=%async_computation.8 | async-start | bytes 131072 | tf_op jit(solution)/shard_map/psum | solution.py:86
  190.4 7.1 %copy-start.2 = (bf16[1,256,2048]{2,1,0:T(8,128)(2,1)S(1)}, bf16[1,256,2048]{2,1,0:T(8,128)(2,1)}, u32[]{:S(2)}) copy-start(bf16[1,256,2048]{2,1,0:T(8,128)(2,1)} %param.8) | copy-start | bytes 3145732
  194.5 115.5 %all-gather.4.cloned.1.call-start = ((), (), s32[]{:S(2)}) async-start(), calls=%async_computation.5 | async-start | bytes 5242880 | tf_op jit(solution)/shard_map/all_gather | solution.py:52
  195.3 145.0 %reduce-scatter.8.cloned.1.call-start = ((), (), s32[]{:S(2)}) async-start(), calls=%async_computation.9 | async-start | bytes 1310720 | tf_op jit(solution)/shard_map/reduce_scatter | solution.py:117
  238.2 192.4 %reduce-scatter.6.cloned.1.call-start = ((), (), s32[]{:S(2)}) async-start(), calls=%async_computation.7 | async-start | bytes 11403264 | tf_op jit(solution)/shard_map/reduce_scatter | solution.py:57
  338.3 0.7 copy-start.4
  338.4 105.3 %reduce-scatter.10.cloned.1.call-start = ((), (), s32[]{:S(2)}) async-start(), calls=%async_computation.10 | async-start | bytes 786432
  409.7 82.9 %all-reduce.6.cloned.1.call-start = ((), (), s32[]{:S(2)}) async-start(), calls=%async_computation.11 | async-start | bytes 3670016
  494.7 17.6 %all-to-all-start.1 = ((bf16[4,3584,16]{1,2,0:T(8,128)(2,1)}), bf16[4,3584,16]{1,2,0:T(8,128)(2,1)S(1)}, u32[]{:S(2)}, u32[]{:S(2)}) async-start(bf16[4,3584,16]{1,2,0:T(8,128)(2,1)} %copy.80), calls=%async_computation.2 | async-start | bytes 917504 | tf_op jit(solution)/shard_map/all_to_all | solution.py:101
  499.3 14.9 %copy-start.1 = (s32[1,4,2]{1,2,0:T(2,128)S(1)}, s32[1,4,2]{1,2,0:T(2,128)}, u32[]{:S(2)}) copy-start(s32[1,4,2]{1,2,0:T(2,128)} %param.12) | copy-start | bytes 100
Sparse Core Ops, SparseCore 0:
  116.9 47.6 all-gather.5
  194.6 33.1 all-reduce.3
  229.5 80.4 all-gather.3
  312.8 25.6 reduce-scatter.7
  340.7 89.8 reduce-scatter.5
  433.4 7.9 reduce-scatter.9
  444.3 48.2 all-reduce.5
where the time goes:
time: 523 us; the launch traced here: 521 us
  waiting for transfers between devices  187 us (36%)
  local copies, waits for them, and re-layouts  150 us (29%)
  other arithmetic  93.6 us (18%)
  matrix products  45.2 us (9%)
  blocking collectives  18.9 us (4%)
  between operations  15 us (3%)
  starting transfers between devices  11.4 us (2%)
    unnamed x22, local copies, waits for them, and re-layouts  135 us
    unnamed x1, other arithmetic  79.7 us
    all_gather x1, waiting for transfers between devices, shards(): lax.all_gather((cotangent, adjoint_local[None]), 'fsdp', axis=1, tiled=True)  71.8 us
    all_to_all x1, waiting for transfers between devices, shards(): lax.all_to_all(adapter_first_factor, 'fsdp', split_axis=1, concat_axis=0,...  58.3 us
    dot_general x1, matrix products, shards(): jnp.einsum('bnd,fd->bnf', rows_up, down_projection_weight, preferred_elem...  21.7 us
    reduce_scatter x1, waiting for transfers between devices, shards(): lax.psum_scatter(joined.astype(jnp.bfloat16), 'tp', scatter_dimension=1,...  20.6 us
    psum x1, waiting for transfers between devices, shards(): latent_rows = lax.psum(latent_part.astype(jnp.bfloat16), 'fsdp')  16.1 us
    unnamed x9, waiting for transfers between devices  13.9 us
  transfers between devices with their start and end apart: 9, of which 6 were waited for; matrix products, arithmetic and copies ran while one was open for 35% of the time, Pallas kernels for 0%

commit v1 on v0

v1 whole, which is shorter than its diff:
```python
import jax
import jax.numpy as jnp
from jax import lax
from jax.sharding import PartitionSpec as P

adapter_scale = 2.0


def take_block(x, pos, count, dim):
    size = x.shape[dim] // count
    return lax.dynamic_slice_in_dim(x, pos * size, size, dim)


def swap(x, axis):
    return lax.ppermute(x, axis, [(0, 1), (1, 0)])


def scatter_sum(x, axis, dim):
    n = lax.axis_size(axis)
    if n != 2:
        return lax.psum_scatter(
            x.astype(jnp.bfloat16), axis, scatter_dimension=dim, tiled=True
        ).astype(jnp.float32)
    pos = lax.axis_index(axis)
    away = take_block(x, 1 - pos, 2, dim).astype(jnp.bfloat16)
    return take_block(x, pos, 2, dim) + swap(away, axis).astype(jnp.float32)


def gather(x, axis, dim):
    n = lax.axis_size(axis)
    if n != 2:
        return lax.all_gather(x, axis, axis=dim, tiled=True)
    other = swap(x, axis)
    first = lax.axis_index(axis) == 0
    return jnp.concatenate(
        [jnp.where(first, x, other), jnp.where(first, other, x)], axis=dim
    )


def base_sum(incoming_gradient, weight):
    rows_up = lax.all_gather(incoming_gradient, "fsdp", axis=0, tiled=True)
    tp = lax.axis_size("tp")
    tp_pos = lax.axis_index("tp")
    dims = (((1,), (1,)), ((), ()))
    if tp != 2:
        base = lax.dot_general(rows_up, weight, dims, preferred_element_type=jnp.float32)
        return lax.psum_scatter(
            base.astype(jnp.bfloat16), "tp", scatter_dimension=0, tiled=True
        ).astype(jnp.float32)
    away = take_block(rows_up, 1 - tp_pos, 2, 0)
    mine = take_block(rows_up, tp_pos, 2, 0)
    arrived = []
    for part in range(4):
        rows = away.shape[0] // 4
        block = lax.dot_general(
            away[part * rows:(part + 1) * rows], weight, dims,
            preferred_element_type=jnp.float32,
        ).astype(jnp.bfloat16)
        arrived.append(swap(block, "tp"))
    own = lax.dot_general(mine, weight, dims, preferred_element_type=jnp.float32)
    own = own.astype(jnp.bfloat16).astype(jnp.float32)
    return own + jnp.concatenate(arrived, axis=0).astype(jnp.float32)


def shards(
    hidden,
    cotangent,
    down_projection_weight,
    adapter_first_factor,
    adapter_second_factor,
    shard_adapter_index,
    member,
):
    fsdp = lax.axis_size("fsdp")
    tp = lax.axis_size("tp")
    sub = lax.axis_size("sub")
    f = lax.axis_index("fsdp")
    t = lax.axis_index("tp")
    s = lax.axis_index("sub")
    rows = cotangent.shape[1]
    rows_all = rows * fsdp
    block_rows = hidden.shape[1]
    units = hidden.shape[2]
    own, _, rank = adapter_first_factor.shape
    adapters = own * fsdp
    up = cotangent[0]
    hid = hidden[0]

    ids = shard_adapter_index[0]
    hits = (
        member[0].reshape(fsdp, rows, -1, 1)
        * (ids[:, None, :, None] == jnp.arange(adapters)).astype(jnp.int32)
    ).sum(axis=2).reshape(rows_all, adapters)
    hits_shard = take_block(hits, f, fsdp, 0)
    hits_block = take_block(hits, t, tp, 0)

    def widen(low, marks):
        return (
            jnp.broadcast_to(low[:, None, :], (low.shape[0], adapters, rank))
            * marks[:, :, None].astype(low.dtype)
        ).reshape(low.shape[0], adapters * rank)

    def narrow(wide, marks):
        return jnp.sum(
            wide.reshape(-1, adapters, rank) * marks[:, :, None].astype(wide.dtype), axis=1
        )

    second = take_block(adapter_second_factor, s, sub, 2)
    second = gather(lax.all_gather(second, "fsdp", axis=0, tiled=True), "sub", 2)
    second = second.reshape(adapters * rank, -1)
    first = take_block(jnp.swapaxes(adapter_first_factor, 1, 2), s, sub, 1)
    first = lax.all_to_all(first, "fsdp", split_axis=2, concat_axis=0, tiled=True)
    first = gather(first, "sub", 1).reshape(adapters * rank, units)

    base = base_sum(up, down_projection_weight)

    qpart = narrow(
        lax.dot_general(up, second, (((1,), (1,)), ((), ())), preferred_element_type=jnp.float32),
        hits_shard,
    ).astype(jnp.bfloat16)
    if tp == 2:
        q = (qpart.astype(jnp.float32) + swap(qpart, "tp").astype(jnp.float32)).astype(jnp.bfloat16)
    else:
        q = lax.psum(qpart, "tp")
    q_all = lax.all_gather(q, "fsdp", axis=0, tiled=True)
    q_wide = widen(take_block(q_all, t, tp, 0), hits_block)

    u = narrow(
        lax.dot_general(hid, first, (((1,), (1,)), ((), ())), preferred_element_type=jnp.float32),
        hits_block,
    ).astype(jnp.bfloat16)
    u = gather(lax.psum(u, "fsdp"), "tp", 0)
    u_wide = widen(take_block(u, f, fsdp, 0), hits_shard)

    part_a = adapter_scale * lax.dot_general(
        q_wide, hid, (((0,), (0,)), ((), ())), preferred_element_type=jnp.float32
    )
    part_a = part_a.reshape(adapters, tp, sub, rank // (tp * sub), units)
    part_a = scatter_sum(scatter_sum(part_a, "sub", 2), "tp", 1)
    part_a = part_a.reshape(adapters, rank // (tp * sub), units).astype(jnp.bfloat16)
    grad_a = lax.all_to_all(part_a, "fsdp", split_axis=0, concat_axis=2, tiled=True)
    grad_a = jnp.swapaxes(grad_a.astype(jnp.float32), 1, 2)

    part_b = adapter_scale * lax.dot_general(
        u_wide, up, (((0,), (0,)), ((), ())), preferred_element_type=jnp.float32
    )
    part_b = scatter_sum(part_b, "sub", 1).astype(jnp.bfloat16)
    grad_b = lax.psum_scatter(part_b, "fsdp", scatter_dimension=0, tiled=True)
    grad_b = grad_b.reshape(own, rank, -1).astype(jnp.float32)

    low = lax.dot_general(
        q_wide, first, (((1,), (0,)), ((), ())), preferred_element_type=jnp.float32
    )
    hidden_gradient = (base + adapter_scale * low).astype(jnp.bfloat16)[None]
    return (hidden_gradient, grad_a, grad_b)


def solution(mesh):
    placed = (
        P(("groups", "sub"), "tp", "fsdp"),
        P(("groups", "sub"), "fsdp", "tp"),
        P("fsdp", "tp"),
        P("fsdp", None, None),
        P("fsdp", None, "tp"),
        P(("groups", "sub"), None, None),
        P(("groups", "sub"), None, None),
    )
    return jax.shard_map(
        shards,
        mesh=mesh,
        in_specs=placed,
        out_specs=(
            P(("groups", "sub"), "tp", "fsdp"),
            P(("groups", "fsdp"), None, ("tp", "sub")),
            P(("groups", "fsdp"), None, ("tp", "sub")),
        ),
        check_vma=False,
    )
```

time: 523 us -> 447 us (0.85)
  local copies, waits for them, and re-layouts: 150 us -> 53 us
  blocking collectives: 18.9 us -> 58.6 us
  waiting for transfers between devices: 187 us -> 152 us
  matrix products: 45.2 us -> 63.6 us
    unnamed x22 -> x29, local copies, waits for them, and re-layouts: 135 us -> 37.1 us
    ppermute x0 -> x11, waiting for transfers between devices: none -> 54.9 us  [swap(): return lax.ppermute(x, axis, [(0, 1), (1, 0)])]
    all_to_all x2 -> x1, waiting for transfers between devices: 64.3 us -> 24.3 us  [shards(): lax.all_to_all(part_a, 'fsdp', split_axis=0, concat_axis=2, tiled=True)]
    all_gather x2 -> x1, waiting for transfers between devices: 71.8 us -> 39.5 us  [base_sum(): rows_up = lax.all_gather(incoming_gradient, 'fsdp', axis=0, tiled=True)]
    all_to_all x0 -> x1, blocking collectives: none -> 29 us  [shards(): lax.all_to_all(first, 'fsdp', split_axis=2, concat_axis=0, tiled=True)]
    reduce_scatter x2 -> x1, waiting for transfers between devices: 20.6 us -> 0.01 us  [shards(): grad_b = lax.psum_scatter(part_b, 'fsdp', scatter_dimension=0, tiled=True)]
    dot_general x8 -> x10, matrix products: 45.2 us -> 63.6 us  [the longest x4 42.9 us: base_sum(): lax.dot_general(away[part * rows:(part + 1) * rows], weight, dims, prefer...]
    psum x1, waiting for transfers between devices: 16.1 us -> 33.2 us  [shards(): u = gather(lax.psum(u, 'fsdp'), 'tp', 0)]
  transfers between devices with their start and end apart: 9 -> 15, of which waited for: 6 -> 10; matrix products, arithmetic and copies ran while one was open for 35% -> 13% of each run, Pallas kernels for 0% -> 0%
where the time goes in v1:
time: 447 us; the launch traced here: 446 us
  waiting for transfers between devices  152 us (34%)
  other arithmetic  91 us (20%)
  matrix products  63.6 us (14%)
  blocking collectives  58.6 us (13%)
  local copies, waits for them, and re-layouts  53 us (12%)
  between operations  14.1 us (3%)
  starting transfers between devices  13.4 us (3%)
    unnamed x2, other arithmetic  79.8 us
    ppermute x11, waiting for transfers between devices, swap(): return lax.ppermute(x, axis, [(0, 1), (1, 0)])  54.9 us
    dot_general x4, matrix products, base_sum(): lax.dot_general(away[part * rows:(part + 1) * rows], weight, dims, prefer...  42.9 us
    all_gather x1, waiting for transfers between devices, base_sum(): rows_up = lax.all_gather(incoming_gradient, 'fsdp', axis=0, tiled=True)  39.5 us
    unnamed x29, local copies, waits for them, and re-layouts  37.1 us
    psum x1, waiting for transfers between devices, shards(): u = gather(lax.psum(u, 'fsdp'), 'tp', 0)  33.2 us
    all_to_all x1, blocking collectives, shards(): lax.all_to_all(first, 'fsdp', split_axis=2, concat_axis=0, tiled=True)  29 us
    all_to_all x1, waiting for transfers between devices, shards(): lax.all_to_all(part_a, 'fsdp', split_axis=0, concat_axis=2, tiled=True)  24.3 us
  transfers between devices with their start and end apart: 15, of which 10 were waited for; matrix products, arithmetic and copies ran while one was open for 13% of the time, Pallas kernels for 0%

profile of v1, /device:TPU:0, one launch (start us, length us, event | category | flops | bytes accessed | tf_op | source)
XLA Modules:
  0.0 445.6 jit_solution(17916033884879009461)
XLA Ops:
  7.2 1.4 copy-done
  8.7 11.4 %copy.30 = bf16[1,14336,32]{2,0,1:T(2,128)(2,1)} copy(bf16[1,14336,32]{1,2,0:T(8,128)(2,1)S(1)} %constant_dynamic-slice_fusion) | data formatting | bytes 1835008
  20.2 9.7 %bitcast_bitcast_fusion.1 = bf16[14336,1,32]{2,1,0:T(2,128)(2,1)} fusion(bf16[1,14336,32]{2,0,1:T(2,128)(2,1)} %copy.30), kind=kLoop, calls=%fused_computation.64 | loop fusion | bytes 1835008
  29.9 0.5 broadcast.31
  30.4 79.7 %reduce = bf16[14336,32]{1,0:T(8,128)(2,1)} reduce(bf16[14336,1,32]{2,1,0:T(2,128)(2,1)} %bitcast_bitcast_fusion.1, bf16[]{:T(256)} %broadcast.31), dimensions={1}, to_apply=%bitcast_bitcast_fusion.1.reduce_sub_computation | reduce | bytes 1835010
  110.1 5.2 %reshape.109 = bf16[4,2,57344]{2,1,0:T(2,128)(2,1)S(1)} reshape(bf16[14336,32]{1,0:T(8,128)(2,1)} %reduce) | data formatting | bytes 1835008
  115.3 29.0 %all_to_all.27 = bf16[4,2,57344]{2,1,0:T(2,128)(2,1)S(1)} all-to-all(bf16[4,2,57344]{2,1,0:T(2,128)(2,1)S(1)} %reshape.109), channel_id=1, replica_groups=mesh['groups'=2,'fsdp'=4,'tp'=2,'sub'=2] {'fsdp'}, dimensions={0} | all-to-all | bytes 1835008 | tf_op jit(solution)/shard_map/all_to_all | solution.py:112
  144.3 4.9 %reshape.110 = bf16[14336,1,32]{2,1,0:T(2,128)(2,1)} reshape(bf16[4,2,57344]{2,1,0:T(2,128)(2,1)S(1)} %all_to_all.27) | data formatting | bytes 1835008
  149.2 13.7 %copy.27 = bf16[1,32,14336]{2,1,0:T(8,128)(2,1)S(1)} copy(bf16[1,32,14336]{1,0,2:T(2,128)(2,1)} %bitcast.94) | data formatting | bytes 1835008 | tf_op jit(solution)/shard_map/all_to_all | solution.py:112
  163.4 2.3 collective-permute-done.6
  165.6 1.3 broadcast_select_fusion.1
  167.1 0.8 copy-done.6
  167.9 1.1 fusion.3
  169.0 0.7 multiply_reduce_fusion
  169.8 33.2 %all-reduce.2.cloned.1.call-done = bf16[512,64]{0,1:T(8,128)(2,1)} async-done(((bf16[512,64]{0,1:T(8,128)(2,1)}), bf16[512,64]{0,1:T(8,128)(2,1)}) %all-reduce.2.cloned.1.call-update) | async-done | bytes 65552 | tf_op jit(solution)/shard_map/psum | solution.py:132
  203.0 1.5 collective-permute-start.9
  204.5 3.0 collective-permute-done.9
  207.5 0.9 broadcast_select_fusion.4
  208.9 1.3 copy-done.5
  210.2 0.9 dynamic-slice_convert_fusion.1
  211.1 15.9 %all_gather.10 = bf16[4,64,1024]{2,1,0:T(8,128)(2,1)S(1)} all-gather(bf16[1,64,1024]{2,1,0:T(8,128)(2,1)S(1)} %constant_dynamic-slice_fusion.3), channel_id=1, replica_groups=mesh['groups'=2,'fsdp'=4,'tp'=2,'sub'=2] {'fsdp'}, dimensions={0}, use_global_device_ids=true | all-gather | bytes 655360 | tf_op jit(solution)/shard_map/all_gather | solution.py:109
  226.9 2.3 add_convert_fusion
  230.0 1.5 collective-permute-start.5
  231.6 2.4 collective-permute-done.5
  234.0 13.8 %all_gather.11 = bf16[1024,64]{0,1:T(8,128)(2,1)S(1)} all-gather(bf16[256,64]{0,1:T(8,128)(2,1)S(1)} %add_convert_fusion.2), channel_id=1, replica_groups=mesh['groups'=2,'fsdp'=4,'tp'=2,'sub'=2] {'fsdp'}, dimensions={0}, use_global_device_ids=true | all-gather | bytes 163840 | tf_op jit(solution)/shard_map/all_gather | solution.py:125
  247.8 3.2 convolution_multiply_fusion
  251.0 1.8 copy-done.2
  253.0 2.6 collective-permute-done.7
  255.6 2.0 convert_add_fusion
  257.6 1.5 collective-permute-start.8
  259.2 11.2 %collective-permute-done.8 = bf16[4,1,1,16,3584]{4,3,2,1,0:T(8,128)(2,1)} collective-permute-done((bf16[4,1,1,16,3584]{4,3,2,1,0:T(8,128)(2,1)S(1)}, bf16[4,1,1,16,3584]{4,3,2,1,0:T(8,128)(2,1)}, u32[]{:S(2)}, u32[]{:S(2)}) %collective-permute-start.8) | collective-permute-done | bytes 458784 | tf_op jit(solution)/shard_map/ppermute | solution.py:15
  270.4 1.9 fusion.11
  272.2 4.4 all-to-all-start.1
  276.6 24.3 %all-to-all-done.1 = bf16[4,16,3584]{2,1,0:T(8,128)(2,1)S(1)} async-done(((bf16[4,16,3584]{2,1,0:T(8,128)(2,1)}), bf16[4,16,3584]{2,1,0:T(8,128)(2,1)S(1)}, u32[]{:S(2)}, u32[]{:S(2)}) %all-to-all-start.1) | async-done | bytes 458784 | tf_op jit(solution)/shard_map/all_to_all | solution.py:141
  301.0 1.0 copy.32
  302.0 1.6 bitcast_convert_fusion
  303.6 39.5 %all-gather.3.cloned.1.call-done = bf16[1,1024,2048]{2,1,0:T(8,128)(2,1)} async-done(((bf16[1,256,2048]{2,1,0:T(8,128)(2,1)}), bf16[1,1024,2048]{2,1,0:T(8,128)(2,1)}) %all-gather.3.cloned.1.call-update) | async-done | bytes 4194320 | tf_op jit(solution)/shard_map/all_gather | solution.py:41
  343.1 10.4 %convolution_convert_fusion.3 = bf16[128,3584]{1,0:T(8,128)(2,1)S(1)} fusion(bf16[3584,2048]{1,0:T(8,128)(2,1)} %param.9, bf16[1,1024,2048]{2,1,0:T(8,128)(2,1)} %all-gather.3.cloned.1.call-done, s32[]{:T(128)S(6)} %add.74), kind=kOutput, calls=%fused_computation.8 | convolution fusion | flops 1879506944 | bytes 16121860 | tf_op jit(solution)/shard_map/dot_general | solution.py:55
  353.5 1.6 collective-permute-start.1
  355.1 10.1 %convolution_convert_fusion.2 = bf16[128,3584]{1,0:T(8,128)(2,1)S(1)} fusion(bf16[3584,2048]{1,0:T(8,128)(2,1)} %param.9, bf16[1,1024,2048]{2,1,0:T(8,128)(2,1)S(1)} %copy-done.8, s32[]{:T(128)S(6)} %add.75), kind=kOutput, calls=%fused_computation.7 | convolution fusion | flops 1879506944 | bytes 16121860 | tf_op jit(solution)/shard_map/dot_general | solution.py:55
  365.2 0.6 collective-permute-start.2
  365.8 11.1 %convolution_convert_fusion.1 = bf16[128,3584]{1,0:T(8,128)(2,1)} fusion(bf16[3584,2048]{1,0:T(8,128)(2,1)} %param.9, bf16[1,1024,2048]{2,1,0:T(8,128)(2,1)S(1)} %copy-done.8, s32[]{:T(128)S(6)} %add.76), kind=kOutput, calls=%fused_computation.6 | convolution fusion | flops 1879506944 | bytes 16121860 | tf_op jit(solution)/shard_map/dot_general | solution.py:55
  376.8 1.5 collective-permute-start.3
  378.4 11.3 %convolution_convert_fusion.4 = bf16[128,3584]{1,0:T(8,128)(2,1)} fusion(bf16[3584,2048]{1,0:T(8,128)(2,1)} %param.9, bf16[1,1024,2048]{2,1,0:T(8,128)(2,1)S(1)} %copy-done.8, s32[]{:T(128)S(6)} %select_n.71), kind=kOutput, calls=%fused_computation.9 | convolution fusion | flops 1879506944 | bytes 16121860 | tf_op jit(solution)/shard_map/dot_general | solution.py:55
  390.2 11.1 %convolution_convert_fusion = bf16[512,3584]{1,0:T(8,128)(2,1)S(1)} fusion(bf16[3584,2048]{1,0:T(8,128)(2,1)} %param.9, bf16[1,1024,2048]{2,1,0:T(8,128)(2,1)S(1)} %copy-done.8, s32[]{:T(128)S(6)} %select_n.70), kind=kOutput, calls=%fused_computation.3 | convolution fusion | flops 7518027776 | bytes 20447236 | tf_op jit(solution)/shard_map/dot_general | solution.py:60
  401.3 14.9 %collective-permute-done.3 = bf16[128,3584]{1,0:T(8,128)(2,1)} collective-permute-done((bf16[128,3584]{1,0:T(8,128)(2,1)}, bf16[128,3584]{1,0:T(8,128)(2,1)}, u32[]{:S(2)}, u32[]{:S(2)}) %collective-permute-start.3) | collective-permute-done | bytes 917536 | tf_op jit(solution)/shard_map/ppermute | solution.py:15
  416.2 18.4 %collective-permute-done = bf16[128,3584]{1,0:T(8,128)(2,1)S(1)} collective-permute-done((bf16[128,3584]{1,0:T(8,128)(2,1)}, bf16[128,3584]{1,0:T(8,128)(2,1)S(1)}, u32[]{:S(2)}, u32[]{:S(2)}) %collective-permute-start) | collective-permute-done | bytes 917536 | tf_op jit(solution)/shard_map/ppermute | solution.py:15
  434.7 4.4 fusion.2
  (58 shorter events, 2.8 us)
Async XLA Ops:
  7.2 1.5 copy-start
  7.2 195.8 %all-reduce.2.cloned.1.call-start = ((), (), s32[]{:S(2)}) async-start(), calls=%async_computation.3 | async-start | bytes 131072 | tf_op jit(solution)/shard_map/psum | solution.py:132
  149.2 13.9 %copy-start.11 = (s32[1,4,2]{1,2,0:T(2,128)S(1)}, s32[1,4,2]{1,2,0:T(2,128)}, u32[]{:S(2)}) copy-start(s32[1,4,2]{1,2,0:T(2,128)} %param.12) | copy-start | bytes 100
  149.2 14.0 %copy-start.10 = (s32[1,1024,2]{1,2,0:T(2,128)S(1)}, s32[1,1024,2]{1,2,0:T(2,128)}, u32[]{:S(2)}) copy-start(s32[1,1024,2]{1,2,0:T(2,128)} %param.13) | copy-start | bytes 24580
  163.0 2.7 collective-permute-start.6
  163.3 4.5 %copy-start.4 = (bf16[1,512,3584]{2,1,0:T(8,128)(2,1)S(1)}, bf16[1,512,3584]{2,1,0:T(8,128)(2,1)}, u32[]{:S(2)}) copy-start(bf16[1,512,3584]{2,1,0:T(8,128)(2,1)} %param.7) | copy-start | bytes 11010052
  166.9 0.9 copy-start.6
  167.9 40.5 %copy-start.3 = (bf16[1,256,2048]{2,1,0:T(8,128)(2,1)S(1)}, bf16[1,256,2048]{2,1,0:T(8,128)(2,1)}, u32[]{:S(2)}) copy-start(bf16[1,256,2048]{2,1,0:T(8,128)(2,1)} %param.8) | copy-start | bytes 3145732
  169.0 42.0 %copy-start.9 = (bf16[1,64,2048]{2,1,0:T(8,128)(2,1)S(1)}, bf16[1,64,2048]{2,1,0:T(8,128)(2,1)}, u32[]{:S(2)}) copy-start(bf16[1,64,2048]{2,1,0:T(8,128)(2,1)} %param.11) | copy-start | bytes 786436
  169.7 132.3 %reduce-scatter.2.cloned.1.call-start = ((), (), s32[]{:S(2)}) async-start(), calls=%async_computation.4 | async-start | bytes 655360 | tf_op jit(solution)/shard_map/reduce_scatter | solution.py:148
  203.0 4.5 %collective-permute-start.9 = (bf16[512,64]{0,1:T(8,128)(2,1)}, bf16[512,64]{0,1:T(8,128)(2,1)S(1)}, u32[]{:S(2)}, u32[]{:S(2)}) collective-permute-start(bf16[512,64]{0,1:T(8,128)(2,1)} %all-reduce.2.cloned.1.call-done), channel_id=1, source_target_pairs={{0,2},{2,0},{1,3},{3,1},{4,6},{6,4},{5,7},{7,5},{8,10},{10,8},{9,1... | collective-permute-start | bytes 196616 | tf_op jit(solution)/shard_map/ppermute | solution.py:15
  208.8 1.3 copy-start.5
  211.0 15.9 %collective-permute-start.10 = (bf16[256,1024]{1,0:T(8,128)(2,1)}, bf16[256,1024]{1,0:T(8,128)(2,1)}, u32[]{:S(2)}, u32[]{:S(2)}) collective-permute-start(bf16[256,1024]{1,0:T(8,128)(2,1)} %dynamic-slice_convert_fusion.1), channel_id=1, source_target_pairs={{0,1},{1,0},{2,3},{3,2},{4,5},{5,4},{6,7},{7,6},{8,9},{9,8},{10,11... | collective-permute-start | bytes 1572872 | tf_op jit(solution)/shard_map/ppermute | solution.py:15
  226.9 2.4 collective-permute-start.4
  229.3 113.8 %all-gather.3.cloned.1.call-start = ((), (), s32[]{:S(2)}) async-start(), calls=%async_computation.5 | async-start | bytes 5242880 | tf_op jit(solution)/shard_map/all_gather | solution.py:41
  230.0 4.0 collective-permute-start.5
  251.0 1.8 copy-start.2
  252.9 2.7 collective-permute-start.7
  257.6 12.7 %collective-permute-start.8 = (bf16[4,1,1,16,3584]{4,3,2,1,0:T(8,128)(2,1)S(1)}, bf16[4,1,1,16,3584]{4,3,2,1,0:T(8,128)(2,1)}, u32[]{:S(2)}, u32[]{:S(2)}) collective-permute-start(bf16[4,1,1,16,3584]{4,3,2,1,0:T(8,128)(2,1)S(1)} %dynamic-slice_convert_fusion.2), channel_id=1, source_target_pairs={{0,2},{2,0},{1,3},{3,1},{4,6},{6,4},{5,7},{7,5},{8,10},{10,8},{9,1... | collective-permute-start | bytes 1376264 | tf_op jit(solution)/shard_map/ppermute | solution.py:15
  272.2 28.7 %all-to-all-start.1 = ((bf16[4,16,3584]{2,1,0:T(8,128)(2,1)}), bf16[4,16,3584]{2,1,0:T(8,128)(2,1)S(1)}, u32[]{:S(2)}, u32[]{:S(2)}) async-start(bf16[4,16,3584]{2,1,0:T(8,128)(2,1)} %fusion.11), calls=%async_computation.1 | async-start | bytes 917504 | tf_op jit(solution)/shard_map/all_to_all | solution.py:141
  343.1 12.0 %copy-start.8 = (bf16[1,1024,2048]{2,1,0:T(8,128)(2,1)S(1)}, bf16[1,1024,2048]{2,1,0:T(8,128)(2,1)}, u32[]{:S(2)}) copy-start(bf16[1,1024,2048]{2,1,0:T(8,128)(2,1)} %all-gather.3.cloned.1.call-done) | copy-start | bytes 12582916
  353.5 47.8 %collective-permute-start.1 = (bf16[128,3584]{1,0:T(8,128)(2,1)S(1)}, bf16[128,3584]{1,0:T(8,128)(2,1)}, u32[]{:S(2)}, u32[]{:S(2)}) collective-permute-start(bf16[128,3584]{1,0:T(8,128)(2,1)S(1)} %convolution_convert_fusion.3), channel_id=1, source_target_pairs={{0,2},{2,0},{1,3},{3,1},{4,6},{6,4},{5,7},{7,5},{8,10},{10,8},{9,1... | collective-permute-start | bytes 2752520 | tf_op jit(solution)/shard_map/ppermute | solution.py:15
  365.2 36.1 %collective-permute-start.2 = (bf16[128,3584]{1,0:T(8,128)(2,1)S(1)}, bf16[128,3584]{1,0:T(8,128)(2,1)}, u32[]{:S(2)}, u32[]{:S(2)}) collective-permute-start(bf16[128,3584]{1,0:T(8,128)(2,1)S(1)} %convolution_convert_fusion.2), channel_id=1, source_target_pairs={{0,2},{2,0},{1,3},{3,1},{4,6},{6,4},{5,7},{7,5},{8,10},{10,8},{9,1... | collective-permute-start | bytes 2752520 | tf_op jit(solution)/shard_map/ppermute | solution.py:15
  376.8 39.4 %collective-permute-start.3 = (bf16[128,3584]{1,0:T(8,128)(2,1)}, bf16[128,3584]{1,0:T(8,128)(2,1)}, u32[]{:S(2)}, u32[]{:S(2)}) collective-permute-start(bf16[128,3584]{1,0:T(8,128)(2,1)} %convolution_convert_fusion.1), channel_id=1, source_target_pairs={{0,2},{2,0},{1,3},{3,1},{4,6},{6,4},{5,7},{7,5},{8,10},{10,8},{9,1... | collective-permute-start | bytes 2752520 | tf_op jit(solution)/shard_map/ppermute | solution.py:15
  389.6 45.0 %copy-start.7 = (bf16[4,32,3584]{2,1,0:T(8,128)(2,1)S(1)}, bf16[4,32,3584]{2,1,0:T(8,128)(2,1)}, u32[]{:S(2)}) copy-start(bf16[4,32,3584]{2,1,0:T(8,128)(2,1)} %copy-done.6) | copy-start | bytes 2752516
  389.7 45.0 %collective-permute-start = (bf16[128,3584]{1,0:T(8,128)(2,1)}, bf16[128,3584]{1,0:T(8,128)(2,1)S(1)}, u32[]{:S(2)}, u32[]{:S(2)}) collective-permute-start(bf16[128,3584]{1,0:T(8,128)(2,1)} %convolution_convert_fusion.4), channel_id=1, source_target_pairs={{0,2},{2,0},{1,3},{3,1},{4,6},{6,4},{5,7},{7,5},{8,10},{10,8},{9,1... | collective-permute-start | bytes 2752520 | tf_op jit(solution)/shard_map/ppermute | solution.py:15
  434.7 4.4 copy-start.1
Sparse Core Ops, SparseCore 0:
  169.8 33.0 all-reduce.1
  229.4 22.6 reduce-scatter.1
  253.7 89.3 all-gather.2

commit v2 on v1

--- a/solution.py
+++ b/solution.py
@@ -1,6 +1,8 @@
 import jax
 import jax.numpy as jnp
 from jax import lax
+from jax.experimental import pallas as pl
+from jax.experimental.pallas import tpu as pltpu
 from jax.sharding import PartitionSpec as P
 
 adapter_scale = 2.0
@@ -37,29 +39,158 @@
     )
 
 
-def base_sum(incoming_gradient, weight):
-    rows_up = lax.all_gather(incoming_gradient, "fsdp", axis=0, tiled=True)
-    tp = lax.axis_size("tp")
-    tp_pos = lax.axis_index("tp")
-    dims = (((1,), (1,)), ((), ()))
-    if tp != 2:
-        base = lax.dot_general(rows_up, weight, dims, preferred_element_type=jnp.float32)
-        return lax.psum_scatter(
-            base.astype(jnp.bfloat16), "tp", scatter_dimension=0, tiled=True
-        ).astype(jnp.float32)
-    away = take_block(rows_up, 1 - tp_pos, 2, 0)
-    mine = take_block(rows_up, tp_pos, 2, 0)
-    arrived = []
-    for part in range(4):
-        rows = away.shape[0] // 4
-        block = lax.dot_general(
-            away[part * rows:(part + 1) * rows], weight, dims,
-            preferred_element_type=jnp.float32,
-        ).astype(jnp.bfloat16)
-        arrived.append(swap(block, "tp"))
-    own = lax.dot_general(mine, weight, dims, preferred_element_type=jnp.float32)
-    own = own.astype(jnp.bfloat16).astype(jnp.float32)
-    return own + jnp.concatenate(arrived, axis=0).astype(jnp.float32)
+MESH = pl.DeviceIdType.MESH
+TILE = 512
+
+
+def base_kernel(
+    cot_ref, w_ref, own_ref, arr_ref,
+    held, weight, stage, own_sem, w_sem, recv_sem, right_sem, left_sem, out_sem, in_sem,
+):
+    f = lax.axis_index("fsdp")
+    t = lax.axis_index("tp")
+    rows = cot_ref.shape[0]
+    tiles = w_ref.shape[0] // TILE
+
+    load = pltpu.make_async_copy(cot_ref, held.at[f], own_sem)
+    load.start()
+    barrier = pltpu.get_barrier_semaphore()
+    for peer in ({"fsdp": (f + 1) % 4}, {"fsdp": (f + 3) % 4}, {"tp": 1 - t}):
+        pl.semaphore_signal(barrier, inc=1, device_id=peer, device_id_type=MESH)
+    pl.semaphore_wait(barrier, 3)
+    load.wait()
+
+    def rightward(p):
+        return pltpu.make_async_remote_copy(
+            held.at[p], held.at[p], right_sem.at[p], recv_sem.at[p],
+            device_id={"fsdp": (f + 1) % 4}, device_id_type=MESH,
+        )
+
+    def leftward(p):
+        return pltpu.make_async_remote_copy(
+            held.at[p], held.at[p], left_sem.at[p], recv_sem.at[p],
+            device_id={"fsdp": (f + 3) % 4}, device_id_type=MESH,
+        )
+
+    def across(slot):
+        return pltpu.make_async_remote_copy(
+            stage.at[slot], arr_ref.at[slot], out_sem.at[slot], in_sem.at[slot],
+            device_id={"tp": 1 - t}, device_id_type=MESH,
+        )
+
+    def w_copy(tile):
+        span = pl.ds(pl.multiple_of(tile * TILE, TILE), TILE)
+        return pltpu.make_async_copy(w_ref.at[span], weight.at[span], w_sem.at[tile])
+
+    upper = f // 2
+    near = f + upper * (3 - 2 * f)
+
+    def step(i, carry):
+        middle = ((i + 1) % 3) * (1 - i // 3) + 3 * (i // 3)
+        p = (1 - near) * i + near * middle
+        p = p + upper * (3 - 2 * p)
+
+        @pl.when(i > 0)
+        def _():
+            rightward(p).wait_recv()
+
+        @pl.when((p <= f) & (f < 3))
+        def _():
+            rightward(p).start()
+
+        @pl.when((p >= f) & (f > 0))
+        def _():
+            leftward(p).start()
+
+        @pl.when(i == 0)
+        def _():
+            lax.fori_loop(0, tiles, lambda k, c: (w_copy(k).start(), c)[1], 0)
+
+        slot = p % 2
+        mine = (p // 2) == t
+
+        def tile_step(k, c):
+            @pl.when(i == 0)
+            def _():
+                w_copy(k).wait()
+
+            span = pl.ds(pl.multiple_of(k * TILE, TILE), TILE)
+            block = lax.dot_general(
+                held[p], weight[span, :], (((1,), (1,)), ((), ())),
+                preferred_element_type=jnp.float32,
+            ).astype(jnp.bfloat16)
+
+            @pl.when(mine)
+            def _():
+                own_ref[slot, :, span] = block
+
+            @pl.when(jnp.logical_not(mine))
+            def _():
+                stage[slot, :, span] = block
+            return c
+
+        lax.fori_loop(0, tiles, tile_step, 0)
+
+        @pl.when(jnp.logical_not(mine))
+        def _():
+            across(slot).start()
+        return carry
+
+    lax.fori_loop(0, 4, step, 0)
+
+    def drain(p, c):
+        @pl.when((p <= f) & (f < 3))
+        def _():
+            rightward(p).wait_send()
+
+        @pl.when((p >= f) & (f > 0))
+        def _():
+            leftward(p).wait_send()
+        return c
+
+    lax.fori_loop(0, 4, drain, 0)
+    for slot in range(2):
+        across(slot).wait()
+
+
+def base_parts(up, weight):
+    rows, width = up.shape
+    units = weight.shape[0]
+    fsdp, tp = lax.axis_size("fsdp"), lax.axis_size("tp")
+    if fsdp == 4 and tp == 2 and units % TILE == 0:
+        half = jax.ShapeDtypeStruct((2, rows, units), jnp.bfloat16)
+        own, arrived = pl.pallas_call(
+            base_kernel,
+            out_shape=(half, half),
+            in_specs=[pl.BlockSpec(memory_space=pl.ANY)] * 2,
+            out_specs=[pl.BlockSpec(memory_space=pltpu.VMEM)] * 2,
+            scratch_shapes=[
+                pltpu.VMEM((4, rows, width), jnp.bfloat16),
+                pltpu.VMEM((units, width), jnp.bfloat16),
+                pltpu.VMEM((2, rows, units), jnp.bfloat16),
+                pltpu.SemaphoreType.DMA,
+                pltpu.SemaphoreType.DMA((units // TILE,)),
+                pltpu.SemaphoreType.DMA((4,)),
+                pltpu.SemaphoreType.DMA((4,)),
+                pltpu.SemaphoreType.DMA((4,)),
+                pltpu.SemaphoreType.DMA((2,)),
+                pltpu.SemaphoreType.DMA((2,)),
+            ],
+            compiler_params=pltpu.CompilerParams(
+                collective_id=0, has_side_effects=True, vmem_limit_bytes=48 * 2**20
+            ),
+            cost_estimate=pl.CostEstimate(
+                flops=8 * rows * width * units,
+                bytes_accessed=2 * units * width + 8 * rows * units,
+                transcendentals=0,
+            ),
+        )(up, weight)
+        return own.reshape(2 * rows, units), arrived.reshape(2 * rows, units)
+    rows_up = lax.all_gather(up, "fsdp", axis=0, tiled=True)
+    base = lax.dot_general(
+        rows_up, weight, (((1,), (1,)), ((), ())), preferred_element_type=jnp.float32
+    )
+    return (lax.psum_scatter(base.astype(jnp.bfloat16), "tp", scatter_dimension=0, tiled=True),)
 
 
 def shards(
@@ -109,10 +240,13 @@
     second = gather(lax.all_gather(second, "fsdp", axis=0, tiled=True), "sub", 2)
     second = second.reshape(adapters * rank, -1)
     first = take_block(jnp.swapaxes(adapter_first_factor, 1, 2), s, sub, 1)
-    first = lax.all_to_all(first, "fsdp", split_axis=2, concat_axis=0, tiled=True)
+    first = jnp.concatenate([first[:, :, k * units:(k + 1) * units] for k in range(fsdp)], axis=0)
+    first = lax.all_to_all(
+        first.reshape(fsdp, own, rank // sub, units), "fsdp", split_axis=0, concat_axis=0
+    ).reshape(adapters, rank // sub, units)
     first = gather(first, "sub", 1).reshape(adapters * rank, units)
 
-    base = base_sum(up, down_projection_weight)
+    base = sum(x.astype(jnp.float32) for x in base_parts(up, down_projection_weight))
 
     qpart = narrow(
         lax.dot_general(up, second, (((1,), (1,)), ((), ())), preferred_element_type=jnp.float32),

time: 447 us -> 309 us (0.69)
  Pallas kernels: 0 us -> 155 us
  waiting for transfers between devices: 152 us -> 56.4 us
  other arithmetic: 91 us -> 18.7 us
  matrix products: 63.6 us -> 11.7 us
  local copies, waits for them, and re-layouts: 53 us -> 7.59 us
  blocking collectives: 58.6 us -> 30.8 us
    pallas_call x0 -> x1, Pallas kernels: none -> 155 us  [base_parts(): pl.pallas_call(base_kernel, out_shape=(half, half), in_specs=[pl.BlockSpe...]
    unnamed x2 -> x1, other arithmetic: 79.8 us -> 0.06 us
    dot_general x5 -> x0, matrix products: 54 us -> none  [the longest x4 42.9 us: base_sum(): lax.dot_general(away[part * rows:(part + 1) * rows], weight, dims, prefer...]
    ppermute x11 -> x7, waiting for transfers between devices: 54.9 us -> 8.46 us  [swap(): return lax.ppermute(x, axis, [(0, 1), (1, 0)])]
    all_gather x1 -> x0, waiting for transfers between devices: 39.5 us -> none  [base_sum(): rows_up = lax.all_gather(incoming_gradient, 'fsdp', axis=0, tiled=True)]
    unnamed x29 -> x22, local copies, waits for them, and re-layouts: 37.1 us -> 3.3 us
    all_to_all x1 -> x0, blocking collectives: 29 us -> none  [shards(): lax.all_to_all(first, 'fsdp', split_axis=2, concat_axis=0, tiled=True)]
    all_to_all x1, waiting for transfers between devices: 24.3 us -> 1.85 us  [shards(): lax.all_to_all(part_a, 'fsdp', split_axis=0, concat_axis=2, tiled=True)]
  transfers between devices with their start and end apart: 15 -> 11, of which waited for: 10 -> 6; matrix products, arithmetic and copies ran while one was open for 13% -> 10% of each run, Pallas kernels for 0% -> 50%
where the time goes in v2:
time: 309 us; the launch traced here: 308 us
  Pallas kernels  155 us (50%)
  waiting for transfers between devices  56.4 us (18%)
  blocking collectives  30.8 us (10%)
  other arithmetic  18.7 us (6%)
  between operations  14.3 us (5%)
  starting transfers between devices  14.1 us (5%)
  matrix products  11.7 us (4%)
  local copies, waits for them, and re-layouts  7.59 us (2%)
    pallas_call x1, Pallas kernels, base_parts(): pl.pallas_call(base_kernel, out_shape=(half, half), in_specs=[pl.BlockSpe...  155 us
    psum x1, waiting for transfers between devices, shards(): u = gather(lax.psum(u, 'fsdp'), 'tp', 0)  31.9 us
    all_gather x1, blocking collectives, shards(): lax.all_gather(second, 'fsdp', axis=0, tiled=True)  17.4 us
    reduce_scatter x1, waiting for transfers between devices, shards(): grad_b = lax.psum_scatter(part_b, 'fsdp', scatter_dimension=0, tiled=True)  14.1 us
    all_gather x1, blocking collectives, shards(): q_all = lax.all_gather(q, 'fsdp', axis=0, tiled=True)  13.4 us
    ppermute x7, waiting for transfers between devices, swap(): return lax.ppermute(x, axis, [(0, 1), (1, 0)])  8.46 us
    dot_general x1, matrix products, shards(): lax.dot_general(q_wide, first, (((1,), (0,)), ((), ())), preferred_elemen...  6.48 us
  transfers between devices with their start and end apart: 11, of which 6 were waited for; matrix products, arithmetic and copies ran while one was open for 10% of the time, Pallas kernels for 50%

profile of v2, /device:TPU:0, one launch (start us, length us, event | category | flops | bytes accessed | tf_op | source)
XLA Modules:
  0.0 308.3 jit_solution(3440114884072463638)
XLA Ops:
  7.2 1.0 constant_dynamic-slice_fusion.1
  8.2 17.4 %all_gather.6 = bf16[4,64,1024]{2,1,0:T(8,128)(2,1)S(1)} all-gather(bf16[1,64,1024]{2,1,0:T(8,128)(2,1)S(1)} %constant_dynamic-slice_fusion.1), channel_id=1, replica_groups=mesh['groups'=2,'fsdp'=4,'tp'=2,'sub'=2] {'fsdp'}, dimensions={0}, use_global_device_ids=true | all-gather | bytes 655360 | tf_op jit(solution)/shard_map/all_gather | solution.py:240
  25.6 0.1 dynamic-slice_bitcast_fusion
  25.7 0.1 fusion.11
  25.7 1.0 maximum_bitcast_fusion
  26.8 5.4 %all-to-all-start = ((bf16[4,1,32,3584]{3,2,1,0:T(8,128)(2,1)}), bf16[4,1,32,3584]{3,2,1,0:T(8,128)(2,1)}, u32[]{:S(2)}, u32[]{:S(2)}) async-start(bf16[4,1,32,3584]{3,2,1,0:T(8,128)(2,1)} %maximum_bitcast_fusion), calls=%async_computation | async-start | bytes 1835008 | tf_op jit(solution)/shard_map/all_to_all | solution.py:244
  32.2 154.7 %shard_map.94 = (bf16[2,256,3584]{2,1,0:T(8,128)(2,1)S(1)}, bf16[2,256,3584]{2,1,0:T(8,128)(2,1)}) custom-call(bf16[256,2048]{1,0:T(8,128)(2,1)S(1)} %bitcast.63, bf16[3584,2048]{1,0:T(8,128)(2,1)} %w_ref.1), custom_call_target="tpu_custom_call" | custom-call | flops 15032385536 | bytes 22020096 | tf_op jit(solution)/shard_map/pallas_call | solution.py:162
  186.9 6.1 %convert_add_fusion = f32[2,256,3584]{2,1,0:T(8,128)} fusion(bf16[2,256,3584]{2,1,0:T(8,128)(2,1)} %get-tuple-element.6, bf16[2,256,3584]{2,1,0:T(8,128)(2,1)S(1)} %get-tuple-element.5), kind=kLoop, calls=%fused_computation.3 | loop fusion | flops 5505024 | bytes 14680064 | tf_op jit(solution)/shard_map/add | solution.py:249
  193.0 0.1 copy.21
  193.1 0.1 compare_convert_fusion
  193.2 0.1 multiply_reduce_fusion.2
  193.3 1.1 broadcast_select_fusion.3
  194.4 0.1 pad_maximum_fusion.1
  194.5 0.5 fusion.9
  195.0 2.5 collective-permute-start.1
  197.5 1.9 collective-permute-done.1
  199.4 13.4 %all_gather.7 = bf16[1024,64]{0,1:T(8,128)(2,1)S(1)} all-gather(bf16[256,64]{0,1:T(8,128)(2,1)S(1)} %add_convert_fusion.2), channel_id=1, replica_groups=mesh['groups'=2,'fsdp'=4,'tp'=2,'sub'=2] {'fsdp'}, dimensions={0}, use_global_device_ids=true | all-gather | bytes 163840 | tf_op jit(solution)/shard_map/all_gather | solution.py:259
  212.9 0.1 collective-permute-start.2
  213.0 3.2 %convolution_multiply_fusion = f32[256,3584]{1,0:T(8,128)S(1)} fusion(bf16[512,256]{0,1:T(8,128)(2,1)S(1)} %bitcast.68, bf16[1,512,3584]{2,1,0:T(8,128)(2,1)} %param.7), kind=kOutput, calls=%fused_computation.4 | convolution fusion | flops 940441600 | bytes 7602176 | tf_op jit(solution)/shard_map/dot_general | solution.py:269
  216.2 1.8 copy-done.3
  218.0 1.1 dynamic-slice_convert_fusion
  219.1 0.5 collective-permute-start.3
  219.6 1.6 broadcast_select_fusion.1
  221.2 0.1 pad_maximum_fusion
  221.3 0.1 copy-done.4
  221.4 1.1 fusion.3
  222.6 0.7 multiply_reduce_fusion
  223.3 0.0 all-reduce.2.cloned.1.call-update
  223.3 2.0 convert_add_fusion.1
  225.3 31.9 %all-reduce.2.cloned.1.call-done = bf16[512,64]{0,1:T(8,128)(2,1)} async-done(((bf16[512,64]{0,1:T(8,128)(2,1)}), bf16[512,64]{0,1:T(8,128)(2,1)}) %all-reduce.2.cloned.1.call-update) | async-done | bytes 65552 | tf_op jit(solution)/shard_map/psum | solution.py:266
  257.2 1.5 collective-permute-start.5
  258.7 0.6 collective-permute-start.4
  259.4 3.1 %collective-permute-done.5 = bf16[512,64]{0,1:T(8,128)(2,1)S(1)} collective-permute-done((bf16[512,64]{0,1:T(8,128)(2,1)}, bf16[512,64]{0,1:T(8,128)(2,1)S(1)}, u32[]{:S(2)}, u32[]{:S(2)}) %collective-permute-start.5) | collective-permute-done | bytes 65568 | tf_op jit(solution)/shard_map/ppermute | solution.py:17
  262.5 0.9 broadcast_select_fusion.4
  263.4 0.4 convolution_multiply_fusion.1
  263.8 1.3 copy-done.5
  265.1 0.9 dynamic-slice_convert_fusion.1
  266.0 3.5 %collective-permute-done.4 = bf16[4,1,1,16,3584]{4,3,2,1,0:T(8,128)(2,1)S(1)} collective-permute-done((bf16[4,1,1,16,3584]{4,3,2,1,0:T(8,128)(2,1)S(1)}, bf16[4,1,1,16,3584]{4,3,2,1,0:T(8,128)(2,1)S(1)}, u32[]{:S(2)}, u32[]{:S(2)}) %collective-permute-start.4) | collective-permute-done | bytes 458784 | tf_op jit(solution)/shard_map/ppermute | solution.py:17
  269.5 0.8 fusion.6
  270.4 3.5 %all-to-all-start.1 = ((bf16[4,16,3584]{2,1,0:T(8,128)(2,1)}), bf16[4,16,3584]{2,1,0:T(8,128)(2,1)S(1)}, u32[]{:S(2)}, u32[]{:S(2)}) async-start(bf16[4,16,3584]{2,1,0:T(8,128)(2,1)} %fusion.6), calls=%async_computation.1 | async-start | bytes 917504 | tf_op jit(solution)/shard_map/all_to_all | solution.py:275
  273.9 2.4 add_convert_fusion
  276.3 0.0 reduce-scatter.2.cloned.1.call-update
  276.3 6.5 %fusion.2 = bf16[1,512,3584]{2,1,0:T(8,128)(2,1)} fusion(f32[2,256,3584]{2,1,0:T(8,128)} %convert_add_fusion, bf16[512,4]{0,1:T(4,128)(2,1)S(1)} %get-tuple-element.18, bf16[512,64]{0,1:T(8,128)(2,1)S(1)} %constant_dynamic-slice_fusion, bf16[4,32,3584]{2,1,0:T(8,128)(2,1)} %copy-done.8, bf16[4,32,3584]{2,1,0:T(8,128)(2,1)S(1)} %copy-done.7), kind=kOutput, calls=%fused_computation.5 | convolution fusion | flops 948830208 | bytes 12914688 | tf_op jit(solution)/shard_map/dot_general | solution.py:285
  282.8 1.8 all-to-all-done.1
  284.7 0.1 convert_bitcast_fusion
  284.7 1.0 copy.23
  285.7 14.1 %reduce-scatter.2.cloned.1.call-done = bf16[64,1024]{1,0:T(8,128)(2,1)} async-done(((bf16[256,1024]{1,0:T(8,128)(2,1)}), bf16[64,1024]{1,0:T(8,128)(2,1)}) %reduce-scatter.2.cloned.1.call-update) | async-done | bytes 131088 | tf_op jit(solution)/shard_map/reduce_scatter | solution.py:282
  299.8 1.6 bitcast_convert_fusion
  (37 shorter events, 0.3 us)
Async XLA Ops:
  7.2 18.4 %copy-start = (bf16[1,14336,64]{1,2,0:T(8,128)(2,1)S(1)}, bf16[1,14336,64]{1,2,0:T(8,128)(2,1)}, u32[]{:S(2)}) copy-start(bf16[1,14336,64]{1,2,0:T(8,128)(2,1)} %param.10) | copy-start | bytes 5505028
  25.6 167.7 %collective-permute-start = (bf16[4,64,1024]{2,1,0:T(8,128)(2,1)S(1)}, bf16[4,64,1024]{2,1,0:T(8,128)(2,1)}, u32[]{:S(2)}, u32[]{:S(2)}) collective-permute-start(bf16[4,64,1024]{2,1,0:T(8,128)(2,1)S(1)} %all_gather.6), channel_id=1, source_target_pairs={{0,1},{1,0},{2,3},{3,2},{4,5},{5,4},{6,7},{7,6},{8,9},{9,8},{10,11... | collective-permute-start | bytes 1572872 | tf_op jit(solution)/shard_map/ppermute | solution.py:17
  25.6 6.6 %copy-start.2 = (bf16[1,256,2048]{2,1,0:T(8,128)(2,1)S(1)}, bf16[1,256,2048]{2,1,0:T(8,128)(2,1)}, u32[]{:S(2)}) copy-start(bf16[1,256,2048]{2,1,0:T(8,128)(2,1)} %param.8) | copy-start | bytes 3145732
  26.8 186.1 %all-to-all-start = ((bf16[4,1,32,3584]{3,2,1,0:T(8,128)(2,1)}), bf16[4,1,32,3584]{3,2,1,0:T(8,128)(2,1)}, u32[]{:S(2)}, u32[]{:S(2)}) async-start(bf16[4,1,32,3584]{3,2,1,0:T(8,128)(2,1)} %maximum_bitcast_fusion), calls=%async_computation | async-start | bytes 1835008 | tf_op jit(solution)/shard_map/all_to_all | solution.py:244
  32.2 225.0 %all-reduce.2.cloned.1.call-start = ((), (), s32[]{:S(2)}) async-start(), calls=%async_computation.3 | async-start | bytes 131072 | tf_op jit(solution)/shard_map/psum | solution.py:266
  186.9 6.1 %copy-start.10 = (s32[1,4,2]{1,2,0:T(2,128)S(1)}, s32[1,4,2]{1,2,0:T(2,128)}, u32[]{:S(2)}) copy-start(s32[1,4,2]{1,2,0:T(2,128)} %param.12) | copy-start | bytes 100
  186.9 6.3 %copy-start.9 = (s32[1,1024,2]{1,2,0:T(2,128)S(1)}, s32[1,1024,2]{1,2,0:T(2,128)}, u32[]{:S(2)}) copy-start(s32[1,1024,2]{1,2,0:T(2,128)} %param.13) | copy-start | bytes 24580
  195.0 4.4 %collective-permute-start.1 = (bf16[256,64]{0,1:T(8,128)(2,1)S(1)}, bf16[256,64]{0,1:T(8,128)(2,1)S(1)}, u32[]{:S(2)}, u32[]{:S(2)}) collective-permute-start(bf16[256,64]{0,1:T(8,128)(2,1)S(1)} %multiply_reduce_fusion.1), channel_id=1, source_target_pairs={{0,2},{2,0},{1,3},{3,1},{4,6},{6,4},{5,7},{7,5},{8,10},{10,8},{9,1... | collective-permute-start | bytes 98312 | tf_op jit(solution)/shard_map/ppermute | solution.py:17
  212.9 6.7 %collective-permute-start.2 = (bf16[4,32,3584]{2,1,0:T(8,128)(2,1)}, bf16[4,32,3584]{2,1,0:T(8,128)(2,1)S(1)}, u32[]{:S(2)}, u32[]{:S(2)}) collective-permute-start(bf16[4,32,3584]{2,1,0:T(8,128)(2,1)} %bitcast.10), channel_id=1, source_target_pairs={{0,1},{1,0},{2,3},{3,2},{4,5},{5,4},{6,7},{7,6},{8,9},{9,8},{10,11... | collective-permute-start | bytes 2752520 | tf_op jit(solution)/shard_map/ppermute | solution.py:17
  216.2 1.8 copy-start.3
  219.1 2.3 copy-start.4
  219.1 4.2 %collective-permute-start.3 = (bf16[4,2,1,16,3584]{4,3,2,1,0:T(8,128)(2,1)}, bf16[4,2,1,16,3584]{4,3,2,1,0:T(8,128)(2,1)}, u32[]{:S(2)}, u32[]{:S(2)}) collective-permute-start(bf16[4,2,1,16,3584]{4,3,2,1,0:T(8,128)(2,1)} %dynamic-slice_convert_fusion), channel_id=1, source_target_pairs={{0,1},{1,0},{2,3},{3,2},{4,5},{5,4},{6,7},{7,6},{8,9},{9,8},{10,11... | collective-permute-start | bytes 2752520 | tf_op jit(solution)/shard_map/ppermute | solution.py:17
  221.2 1.4 copy-start.6
  221.2 1.4 copy-start.8
  257.2 5.2 %collective-permute-start.5 = (bf16[512,64]{0,1:T(8,128)(2,1)}, bf16[512,64]{0,1:T(8,128)(2,1)S(1)}, u32[]{:S(2)}, u32[]{:S(2)}) collective-permute-start(bf16[512,64]{0,1:T(8,128)(2,1)} %all-reduce.2.cloned.1.call-done), channel_id=1, source_target_pairs={{0,2},{2,0},{1,3},{3,1},{4,6},{6,4},{5,7},{7,5},{8,10},{10,8},{9,1... | collective-permute-start | bytes 196616 | tf_op jit(solution)/shard_map/ppermute | solution.py:17
  258.7 10.8 %collective-permute-start.4 = (bf16[4,1,1,16,3584]{4,3,2,1,0:T(8,128)(2,1)S(1)}, bf16[4,1,1,16,3584]{4,3,2,1,0:T(8,128)(2,1)S(1)}, u32[]{:S(2)}, u32[]{:S(2)}) collective-permute-start(bf16[4,1,1,16,3584]{4,3,2,1,0:T(8,128)(2,1)S(1)} %dynamic-slice_convert_fusion.2), channel_id=1, source_target_pairs={{0,2},{2,0},{1,3},{3,1},{4,6},{6,4},{5,7},{7,5},{8,10},{10,8},{9,1... | collective-permute-start | bytes 1376264 | tf_op jit(solution)/shard_map/ppermute | solution.py:17
  263.8 1.3 copy-start.5
  265.1 11.2 %copy-start.7 = (bf16[4,32,3584]{2,1,0:T(8,128)(2,1)S(1)}, bf16[4,32,3584]{2,1,0:T(8,128)(2,1)}, u32[]{:S(2)}) copy-start(bf16[4,32,3584]{2,1,0:T(8,128)(2,1)} %copy-done.6) | copy-start | bytes 2752516
  266.0 7.9 %collective-permute-start.6 = (bf16[256,1024]{1,0:T(8,128)(2,1)}, bf16[256,1024]{1,0:T(8,128)(2,1)}, u32[]{:S(2)}, u32[]{:S(2)}) collective-permute-start(bf16[256,1024]{1,0:T(8,128)(2,1)} %dynamic-slice_convert_fusion.1), channel_id=1, source_target_pairs={{0,1},{1,0},{2,3},{3,2},{4,5},{5,4},{6,7},{7,6},{8,9},{9,8},{10,11... | collective-permute-start | bytes 1572872 | tf_op jit(solution)/shard_map/ppermute | solution.py:17
  270.4 14.3 %all-to-all-start.1 = ((bf16[4,16,3584]{2,1,0:T(8,128)(2,1)}), bf16[4,16,3584]{2,1,0:T(8,128)(2,1)S(1)}, u32[]{:S(2)}, u32[]{:S(2)}) async-start(bf16[4,16,3584]{2,1,0:T(8,128)(2,1)} %fusion.6), calls=%async_computation.1 | async-start | bytes 917504 | tf_op jit(solution)/shard_map/all_to_all | solution.py:275
  273.9 25.9 %reduce-scatter.2.cloned.1.call-start = ((), (), s32[]{:S(2)}) async-start(), calls=%async_computation.4 | async-start | bytes 655360 | tf_op jit(solution)/shard_map/reduce_scatter | solution.py:282
  276.3 25.1 %copy-start.1 = (bf16[1,14336,64]{1,2,0:T(8,128)(2,1)S(1)}, bf16[1,14336,64]{1,2,0:T(8,128)(2,1)}, u32[]{:S(2)}) copy-start(bf16[1,14336,64]{1,2,0:T(8,128)(2,1)} %param.10) | copy-start | bytes 5505028
Sparse Core Ops, SparseCore 0:
  223.4 33.7 all-reduce.1
  277.1 22.6 reduce-scatter.1

commit v3 on v2

--- a/solution.py
+++ b/solution.py
@@ -72,9 +72,11 @@
             device_id={"fsdp": (f + 3) % 4}, device_id_type=MESH,
         )
 
-    def across(slot):
+    def across(slot, tile):
+        span = pl.ds(pl.multiple_of(tile * TILE, TILE), TILE)
         return pltpu.make_async_remote_copy(
-            stage.at[slot], arr_ref.at[slot], out_sem.at[slot], in_sem.at[slot],
+            stage.at[slot, :, span], arr_ref.at[slot, :, span],
+            out_sem.at[slot, tile], in_sem.at[slot, tile],
             device_id={"tp": 1 - t}, device_id_type=MESH,
         )
 
@@ -127,13 +129,10 @@
             @pl.when(jnp.logical_not(mine))
             def _():
                 stage[slot, :, span] = block
+                across(slot, k).start()
             return c
 
         lax.fori_loop(0, tiles, tile_step, 0)
-
-        @pl.when(jnp.logical_not(mine))
-        def _():
-            across(slot).start()
         return carry
 
     lax.fori_loop(0, 4, step, 0)
@@ -150,7 +149,7 @@
 
     lax.fori_loop(0, 4, drain, 0)
     for slot in range(2):
-        across(slot).wait()
+        lax.fori_loop(0, tiles, lambda k, c, slot=slot: (across(slot, k).wait(), c)[1], 0)
 
 
 def base_parts(up, weight):
@@ -173,14 +172,14 @@
                 pltpu.SemaphoreType.DMA((4,)),
                 pltpu.SemaphoreType.DMA((4,)),
                 pltpu.SemaphoreType.DMA((4,)),
-                pltpu.SemaphoreType.DMA((2,)),
-                pltpu.SemaphoreType.DMA((2,)),
+                pltpu.SemaphoreType.DMA((2, units // TILE)),
+                pltpu.SemaphoreType.DMA((2, units // TILE)),
             ],
             compiler_params=pltpu.CompilerParams(
                 collective_id=0, has_side_effects=True, vmem_limit_bytes=48 * 2**20
             ),
             cost_estimate=pl.CostEstimate(
-                flops=8 * rows * width * units,
+                flops=64 * rows * width * units,
                 bytes_accessed=2 * units * width + 8 * rows * units,
                 transcendentals=0,
             ),
@@ -236,17 +235,15 @@
             wide.reshape(-1, adapters, rank) * marks[:, :, None].astype(wide.dtype), axis=1
         )
 
-    second = take_block(adapter_second_factor, s, sub, 2)
-    second = gather(lax.all_gather(second, "fsdp", axis=0, tiled=True), "sub", 2)
-    second = second.reshape(adapters * rank, -1)
     first = take_block(jnp.swapaxes(adapter_first_factor, 1, 2), s, sub, 1)
     first = jnp.concatenate([first[:, :, k * units:(k + 1) * units] for k in range(fsdp)], axis=0)
     first = lax.all_to_all(
         first.reshape(fsdp, own, rank // sub, units), "fsdp", split_axis=0, concat_axis=0
     ).reshape(adapters, rank // sub, units)
     first = gather(first, "sub", 1).reshape(adapters * rank, units)
-
-    base = sum(x.astype(jnp.float32) for x in base_parts(up, down_projection_weight))
+    second = take_block(adapter_second_factor, s, sub, 2)
+    second = gather(lax.all_gather(second, "fsdp", axis=0, tiled=True), "sub", 2)
+    second = second.reshape(adapters * rank, -1)
 
     qpart = narrow(
         lax.dot_general(up, second, (((1,), (1,)), ((), ())), preferred_element_type=jnp.float32),
@@ -259,12 +256,10 @@
     q_all = lax.all_gather(q, "fsdp", axis=0, tiled=True)
     q_wide = widen(take_block(q_all, t, tp, 0), hits_block)
 
-    u = narrow(
+    u_part = narrow(
         lax.dot_general(hid, first, (((1,), (1,)), ((), ())), preferred_element_type=jnp.float32),
         hits_block,
     ).astype(jnp.bfloat16)
-    u = gather(lax.psum(u, "fsdp"), "tp", 0)
-    u_wide = widen(take_block(u, f, fsdp, 0), hits_shard)
 
     part_a = adapter_scale * lax.dot_general(
         q_wide, hid, (((0,), (0,)), ((), ())), preferred_element_type=jnp.float32
@@ -272,9 +267,17 @@
     part_a = part_a.reshape(adapters, tp, sub, rank // (tp * sub), units)
     part_a = scatter_sum(scatter_sum(part_a, "sub", 2), "tp", 1)
     part_a = part_a.reshape(adapters, rank // (tp * sub), units).astype(jnp.bfloat16)
+
+    up_base, u_part, part_a = lax.optimization_barrier((up, u_part, part_a))
+    u = lax.psum(u_part, "fsdp")
     grad_a = lax.all_to_all(part_a, "fsdp", split_axis=0, concat_axis=2, tiled=True)
+    bases = base_parts(up_base, down_projection_weight)
+    bases, u, grad_a = lax.optimization_barrier((bases, u, grad_a))
+    base = sum(x.astype(jnp.float32) for x in bases)
     grad_a = jnp.swapaxes(grad_a.astype(jnp.float32), 1, 2)
 
+    u = gather(u, "tp", 0)
+    u_wide = widen(take_block(u, f, fsdp, 0), hits_shard)
     part_b = adapter_scale * lax.dot_general(
         u_wide, up, (((0,), (0,)), ((), ())), preferred_element_type=jnp.float32
     )

time: 309 us -> 280 us (0.906)
  waiting for transfers between devices: 56.4 us -> 39.8 us
  Pallas kernels: 155 us -> 144 us
  other arithmetic: 18.7 us -> 14.1 us
    psum x1, waiting for transfers between devices: 31.9 us -> 0.01 us  [shards(): u = lax.psum(u_part, 'fsdp')]
    all_to_all x1, waiting for transfers between devices: 0.01 us -> 18.9 us  [shards(): lax.all_to_all(first.reshape(fsdp, own, rank // sub, units), 'fsdp', spli...]
    pallas_call x1, Pallas kernels: 155 us -> 144 us  [base_parts(): pl.pallas_call(base_kernel, out_shape=(half, half), in_specs=[pl.BlockSpe...]
    add x1 -> x0, other arithmetic: 6.09 us -> none  [shards(): sum((x.astype(jnp.float32) for x in base_parts(up, down_projection_weight)))]
  transfers between devices with their start and end apart: 11 -> 11, of which waited for: 6 -> 6; matrix products, arithmetic and copies ran while one was open for 10% -> 6% of each run, Pallas kernels for 50% -> 51%
where the time goes in v3:
time: 280 us; the launch traced here: 279 us
  Pallas kernels  144 us (51%)
  waiting for transfers between devices  39.8 us (14%)
  blocking collectives  31.1 us (11%)
  starting transfers between devices  14.3 us (5%)
  between operations  14.3 us (5%)
  other arithmetic  14.1 us (5%)
  matrix products  12.1 us (4%)
  local copies, waits for them, and re-layouts  9.87 us (4%)
    pallas_call x1, Pallas kernels, base_parts(): pl.pallas_call(base_kernel, out_shape=(half, half), in_specs=[pl.BlockSpe...  144 us
    all_to_all x1, waiting for transfers between devices, shards(): lax.all_to_all(first.reshape(fsdp, own, rank // sub, units), 'fsdp', spli...  18.9 us
    all_gather x1, blocking collectives, shards(): lax.all_gather(second, 'fsdp', axis=0, tiled=True)  17.4 us
    all_gather x1, blocking collectives, shards(): q_all = lax.all_gather(q, 'fsdp', axis=0, tiled=True)  13.7 us
    reduce_scatter x1, waiting for transfers between devices, shards(): grad_b = lax.psum_scatter(part_b, 'fsdp', scatter_dimension=0, tiled=True)  13.6 us
    ppermute x7, waiting for transfers between devices, swap(): return lax.ppermute(x, axis, [(0, 1), (1, 0)])  7.28 us
    dot_general x1, matrix products, shards(): lax.dot_general(q_wide, first, (((1,), (0,)), ((), ())), preferred_elemen...  6.82 us
    ppermute x7, starting transfers between devices, swap(): return lax.ppermute(x, axis, [(0, 1), (1, 0)])  5.67 us
  transfers between devices with their start and end apart: 11, of which 6 were waited for; matrix products, arithmetic and copies ran while one was open for 6% of the time, Pallas kernels for 51%

profile of v3, /device:TPU:0, one launch (start us, length us, event | category | flops | bytes accessed | tf_op | source)
XLA Modules:
  0.0 279.1 jit_solution(17877884410349975943)
XLA Ops:
  7.2 1.1 constant_dynamic-slice_fusion.1
  8.3 17.4 %all_gather.6 = bf16[4,64,1024]{2,1,0:T(8,128)(2,1)S(1)} all-gather(bf16[1,64,1024]{2,1,0:T(8,128)(2,1)S(1)} %constant_dynamic-slice_fusion.1), channel_id=1, replica_groups=mesh['groups'=2,'fsdp'=4,'tp'=2,'sub'=2] {'fsdp'}, dimensions={0}, use_global_device_ids=true | all-gather | bytes 655360 | tf_op jit(solution)/shard_map/all_gather | solution.py:245
  25.6 1.0 dynamic-slice_bitcast_fusion
  26.6 0.8 copy.21
  27.4 0.1 compare_convert_fusion
  27.5 0.8 multiply_reduce_fusion.2
  28.3 1.1 broadcast_select_fusion.3
  29.4 0.1 pad_maximum_fusion.1
  29.5 0.5 fusion.9
  30.0 1.6 collective-permute-start.2
  31.6 2.4 collective-permute-done.2
  34.0 13.7 %all_gather.7 = bf16[1024,64]{0,1:T(8,128)(2,1)S(1)} all-gather(bf16[256,64]{0,1:T(8,128)(2,1)S(1)} %add_convert_fusion.2), channel_id=1, replica_groups=mesh['groups'=2,'fsdp'=4,'tp'=2,'sub'=2] {'fsdp'}, dimensions={0}, use_global_device_ids=true | all-gather | bytes 163840 | tf_op jit(solution)/shard_map/all_gather | solution.py:256
  47.7 3.2 %convolution_multiply_fusion = f32[256,3584]{1,0:T(8,128)S(1)} fusion(bf16[512,256]{0,1:T(8,128)(2,1)S(1)} %bitcast.67, bf16[1,512,3584]{2,1,0:T(8,128)(2,1)} %param.7), kind=kOutput, calls=%fused_computation.3 | convolution fusion | flops 940441600 | bytes 7602176 | tf_op jit(solution)/shard_map/dot_general | solution.py:264
  51.0 1.8 copy-done.3
  52.8 1.1 dynamic-slice_convert_fusion
  53.9 0.1 fusion.11
  54.0 1.0 maximum_bitcast_fusion
  55.0 5.1 %all-to-all-start = ((bf16[4,1,32,3584]{3,2,1,0:T(8,128)(2,1)}), bf16[4,1,32,3584]{3,2,1,0:T(8,128)(2,1)}, u32[]{:S(2)}, u32[]{:S(2)}) async-start(bf16[4,1,32,3584]{3,2,1,0:T(8,128)(2,1)} %maximum_bitcast_fusion), calls=%async_computation | async-start | bytes 1835008 | tf_op jit(solution)/shard_map/all_to_all | solution.py:240
  60.1 2.0 convert_add_fusion
  62.1 1.2 copy-done.5
  63.3 1.6 collective-permute-start.4
  64.9 18.9 %all-to-all-done = bf16[4,1,32,3584]{3,2,1,0:T(8,128)(2,1)} async-done(((bf16[4,1,32,3584]{3,2,1,0:T(8,128)(2,1)}), bf16[4,1,32,3584]{3,2,1,0:T(8,128)(2,1)}, u32[]{:S(2)}, u32[]{:S(2)}) %all-to-all-start) | async-done | bytes 917536 | tf_op jit(solution)/shard_map/all_to_all | solution.py:240
  83.8 2.2 fusion.6
  86.0 0.5 collective-permute-done
  86.5 1.5 broadcast_select_fusion.1
  88.0 0.1 pad_maximum_fusion
  88.2 0.1 copy-done.4
  88.3 1.1 fusion.4
  89.4 0.7 multiply_reduce_fusion
  90.1 0.0 all-reduce.2.cloned.1.call-update
  90.1 3.5 %all-to-all-start.1 = ((bf16[4,16,3584]{2,1,0:T(8,128)(2,1)}), bf16[4,16,3584]{2,1,0:T(8,128)(2,1)S(1)}, u32[]{:S(2)}, u32[]{:S(2)}) async-start(bf16[4,16,3584]{2,1,0:T(8,128)(2,1)} %fusion.6), calls=%async_computation.1 | async-start | bytes 917504 | tf_op jit(solution)/shard_map/all_to_all | solution.py:273
  93.6 0.0 reduce-scatter.2.cloned.1.call-start
  93.7 143.6 %shard_map.94 = (bf16[2,256,3584]{2,1,0:T(8,128)(2,1)S(1)}, bf16[2,256,3584]{2,1,0:T(8,128)(2,1)}) custom-call(bf16[256,2048]{1,0:T(8,128)(2,1)S(1)} %bitcast.59, bf16[3584,2048]{1,0:T(8,128)(2,1)} %w_ref.1), custom_call_target="tpu_custom_call" | custom-call | flops 120259084288 | bytes 22020096 | tf_op jit(solution)/shard_map/pallas_call | solution.py:161
  237.3 1.8 copy-done.2
  239.1 0.8 copy.23
  239.9 2.5 collective-permute-start.5
  242.4 2.5 collective-permute-done.5
  244.8 0.9 broadcast_select_fusion.4
  245.8 0.4 convolution_multiply_fusion.1
  246.2 0.1 dynamic-slice_convert_fusion.1
  246.3 0.1 collective-permute-start.6
  246.4 1.9 collective-permute-done.6
  248.3 0.9 add_convert_fusion
  249.2 0.0 reduce-scatter.2.cloned.1.call-update
  249.3 1.0 convert_bitcast_fusion
  250.3 6.8 %fusion.2 = bf16[1,512,3584]{2,1,0:T(8,128)(2,1)} fusion(bf16[512,3584]{1,0:T(8,128)(2,1)} %bitcast.75, bf16[512,3584]{1,0:T(8,128)(2,1)} %bitcast.60, bf16[512,4]{0,1:T(4,128)(2,1)S(1)} %get-tuple-element.33, bf16[512,64]{0,1:T(8,128)(2,1)S(1)} %constant_dynamic-slice_fusion, bf16[4,32,3584]{2,1,0:T(8,128)(2,1)} %copy-done.9, ...), kind=kOutput, calls=%fused_computation.4 | convolution fusion | flops 954335232 | bytes 12914688 | tf_op jit(solution)/shard_map/dot_general | solution.py:288
  257.1 13.6 %reduce-scatter.2.cloned.1.call-done = bf16[64,1024]{1,0:T(8,128)(2,1)} async-done(((bf16[256,1024]{1,0:T(8,128)(2,1)}), bf16[64,1024]{1,0:T(8,128)(2,1)}) %reduce-scatter.2.cloned.1.call-update) | async-done | bytes 131088 | tf_op jit(solution)/shard_map/reduce_scatter | solution.py:285
  270.7 1.6 bitcast_convert_fusion
  (36 shorter events, 0.3 us)
Async XLA Ops:
  7.2 18.5 %copy-start = (bf16[1,14336,64]{1,2,0:T(8,128)(2,1)S(1)}, bf16[1,14336,64]{1,2,0:T(8,128)(2,1)}, u32[]{:S(2)}) copy-start(bf16[1,14336,64]{1,2,0:T(8,128)(2,1)} %param.10) | copy-start | bytes 5505028
  7.2 22.3 %copy-start.1 = (bf16[1,256,2048]{2,1,0:T(8,128)(2,1)S(1)}, bf16[1,256,2048]{2,1,0:T(8,128)(2,1)}, u32[]{:S(2)}) copy-start(bf16[1,256,2048]{2,1,0:T(8,128)(2,1)} %param.8) | copy-start | bytes 3145732
  25.6 2.6 collective-permute-start.1
  30.0 4.0 %collective-permute-start.2 = (bf16[256,64]{0,1:T(8,128)(2,1)S(1)}, bf16[256,64]{0,1:T(8,128)(2,1)S(1)}, u32[]{:S(2)}, u32[]{:S(2)}) collective-permute-start(bf16[256,64]{0,1:T(8,128)(2,1)S(1)} %multiply_reduce_fusion.1), channel_id=1, source_target_pairs={{0,2},{2,0},{1,3},{3,1},{4,6},{6,4},{5,7},{7,5},{8,10},{10,8},{9,1... | collective-permute-start | bytes 98312 | tf_op jit(solution)/shard_map/ppermute | solution.py:17
  47.7 6.2 %copy-start.6 = (bf16[1,32,14336]{2,1,0:T(8,128)(2,1)S(1)}, bf16[1,32,14336]{2,1,0:T(8,128)(2,1)}, u32[]{:S(2)}) copy-start(bf16[1,32,14336]{2,1,0:T(8,128)(2,1)} %dynamic-slice_bitcast_fusion) | copy-start | bytes 2752516
  51.0 1.8 copy-start.3
  53.9 6.2 %collective-permute-start.3 = (bf16[4,2,1,16,3584]{4,3,2,1,0:T(8,128)(2,1)}, bf16[4,2,1,16,3584]{4,3,2,1,0:T(8,128)(2,1)}, u32[]{:S(2)}, u32[]{:S(2)}) collective-permute-start(bf16[4,2,1,16,3584]{4,3,2,1,0:T(8,128)(2,1)} %dynamic-slice_convert_fusion), channel_id=1, source_target_pairs={{0,1},{1,0},{2,3},{3,2},{4,5},{5,4},{6,7},{7,6},{8,9},{9,8},{10,11... | collective-permute-start | bytes 2752520 | tf_op jit(solution)/shard_map/ppermute | solution.py:17
  55.0 28.8 %all-to-all-start = ((bf16[4,1,32,3584]{3,2,1,0:T(8,128)(2,1)}), bf16[4,1,32,3584]{3,2,1,0:T(8,128)(2,1)}, u32[]{:S(2)}, u32[]{:S(2)}) async-start(bf16[4,1,32,3584]{3,2,1,0:T(8,128)(2,1)} %maximum_bitcast_fusion), calls=%async_computation | async-start | bytes 1835008 | tf_op jit(solution)/shard_map/all_to_all | solution.py:240
  60.1 179.8 %all-reduce.2.cloned.1.call-start = ((), (), s32[]{:S(2)}) async-start(), calls=%async_computation.3 | async-start | bytes 131072 | tf_op jit(solution)/shard_map/psum | solution.py:272
  62.1 1.2 copy-start.5
  63.3 20.4 %collective-permute-start.4 = (bf16[4,1,1,16,3584]{4,3,2,1,0:T(8,128)(2,1)S(1)}, bf16[4,1,1,16,3584]{4,3,2,1,0:T(8,128)(2,1)}, u32[]{:S(2)}, u32[]{:S(2)}) collective-permute-start(bf16[4,1,1,16,3584]{4,3,2,1,0:T(8,128)(2,1)S(1)} %dynamic-slice_convert_fusion.2), channel_id=1, source_target_pairs={{0,2},{2,0},{1,3},{3,1},{4,6},{6,4},{5,7},{7,5},{8,10},{10,8},{9,1... | collective-permute-start | bytes 1376264 | tf_op jit(solution)/shard_map/ppermute | solution.py:17
  83.8 2.7 collective-permute-start
  85.9 2.3 copy-start.4
  88.0 1.4 copy-start.7
  88.0 1.4 copy-start.9
  90.1 149.0 %all-to-all-start.1 = ((bf16[4,16,3584]{2,1,0:T(8,128)(2,1)}), bf16[4,16,3584]{2,1,0:T(8,128)(2,1)S(1)}, u32[]{:S(2)}, u32[]{:S(2)}) async-start(bf16[4,16,3584]{2,1,0:T(8,128)(2,1)} %fusion.6), calls=%async_computation.1 | async-start | bytes 917504 | tf_op jit(solution)/shard_map/all_to_all | solution.py:273
  93.6 177.1 %reduce-scatter.2.cloned.1.call-start = ((), (), s32[]{:S(2)}) async-start(), calls=%async_computation.4 | async-start | bytes 655360 | tf_op jit(solution)/shard_map/reduce_scatter | solution.py:285
  237.3 1.8 copy-start.2
  239.9 4.9 %collective-permute-start.5 = (bf16[512,64]{0,1:T(8,128)(2,1)}, bf16[512,64]{0,1:T(8,128)(2,1)S(1)}, u32[]{:S(2)}, u32[]{:S(2)}) collective-permute-start(bf16[512,64]{0,1:T(8,128)(2,1)} %all-reduce.2.cloned.1.call-done), channel_id=1, source_target_pairs={{0,2},{2,0},{1,3},{3,1},{4,6},{6,4},{5,7},{7,5},{8,10},{10,8},{9,1... | collective-permute-start | bytes 196616 | tf_op jit(solution)/shard_map/ppermute | solution.py:17
  245.7 3.6 %copy-start.10 = (bf16[1,4,2,8,3584]{4,3,1,2,0:T(8,128)(2,1)S(1)}, bf16[1,4,2,8,3584]{4,3,1,2,0:T(8,128)(2,1)}, u32[]{:S(2)}) copy-start(bf16[1,4,2,8,3584]{4,3,1,2,0:T(8,128)(2,1)} %copy.23) | copy-start | bytes 1376260
  246.2 4.0 %copy-start.8 = (bf16[4,32,3584]{2,1,0:T(8,128)(2,1)S(1)}, bf16[4,32,3584]{2,1,0:T(8,128)(2,1)}, u32[]{:S(2)}) copy-start(bf16[4,32,3584]{2,1,0:T(8,128)(2,1)} %copy-done.7) | copy-start | bytes 2752516
  246.3 2.0 collective-permute-start.6
Sparse Core Ops, SparseCore 0:
  90.2 37.5 all-reduce.1
  249.4 21.2 reduce-scatter.1

commit v4 on v3

--- a/solution.py
+++ b/solution.py
@@ -192,6 +192,59 @@
     return (lax.psum_scatter(base.astype(jnp.bfloat16), "tp", scatter_dimension=0, tiled=True),)
 
 
+def factor_kernel(first_ref, second_ref, first_out, second_out, send_sem, recv_sem, own_sem):
+    f = lax.axis_index("fsdp")
+    barrier = pltpu.get_barrier_semaphore()
+    for d in range(1, 4):
+        pl.semaphore_signal(
+            barrier, inc=1, device_id={"fsdp": (f + d) % 4}, device_id_type=MESH
+        )
+    pl.semaphore_wait(barrier, 3)
+    copies = []
+    for d in (1, 2, 3):
+        to = (f + d) % 4
+        for kind, (source, target) in enumerate(
+            ((second_ref, second_out.at[f]), (first_ref.at[to], first_out.at[f]))
+        ):
+            copies.append(
+                pltpu.make_async_remote_copy(
+                    source, target, send_sem.at[kind, d - 1], recv_sem.at[kind, d - 1],
+                    device_id={"fsdp": to}, device_id_type=MESH,
+                )
+            )
+    copies.append(pltpu.make_async_copy(second_ref, second_out.at[f], own_sem.at[0]))
+    copies.append(pltpu.make_async_copy(first_ref.at[f], first_out.at[f], own_sem.at[1]))
+    for copy in copies:
+        copy.start()
+    for copy in copies:
+        copy.wait()
+
+
+def exchange_factors(first, second):
+    fsdp = first.shape[0]
+    if fsdp == 4:
+        vmem = pl.BlockSpec(memory_space=pltpu.VMEM)
+        return pl.pallas_call(
+            factor_kernel,
+            out_shape=(
+                jax.ShapeDtypeStruct(first.shape, first.dtype),
+                jax.ShapeDtypeStruct((fsdp,) + second.shape, second.dtype),
+            ),
+            in_specs=[vmem] * 2,
+            out_specs=[vmem] * 2,
+            scratch_shapes=[
+                pltpu.SemaphoreType.DMA((2, 3)),
+                pltpu.SemaphoreType.DMA((2, 3)),
+                pltpu.SemaphoreType.DMA((2,)),
+            ],
+            compiler_params=pltpu.CompilerParams(
+                collective_id=1, has_side_effects=True, vmem_limit_bytes=24 * 2**20
+            ),
+        )(first, second)
+    first = lax.all_to_all(first, "fsdp", split_axis=0, concat_axis=0)
+    return first, lax.all_gather(second, "fsdp", axis=0)
+
+
 def shards(
     hidden,
     cotangent,
@@ -237,13 +290,13 @@
 
     first = take_block(jnp.swapaxes(adapter_first_factor, 1, 2), s, sub, 1)
     first = jnp.concatenate([first[:, :, k * units:(k + 1) * units] for k in range(fsdp)], axis=0)
-    first = lax.all_to_all(
-        first.reshape(fsdp, own, rank // sub, units), "fsdp", split_axis=0, concat_axis=0
-    ).reshape(adapters, rank // sub, units)
-    first = gather(first, "sub", 1).reshape(adapters * rank, units)
     second = take_block(adapter_second_factor, s, sub, 2)
-    second = gather(lax.all_gather(second, "fsdp", axis=0, tiled=True), "sub", 2)
-    second = second.reshape(adapters * rank, -1)
+    first, second = exchange_factors(
+        first.reshape(fsdp, own * (rank // sub), units), second.reshape(own * rank, -1)
+    )
+    first = gather(first.reshape(adapters, rank // sub, units), "sub", 1)
+    first = first.reshape(adapters * rank, units)
+    second = gather(second.reshape(adapters, rank, -1), "sub", 2).reshape(adapters * rank, -1)
 
     qpart = narrow(
         lax.dot_general(up, second, (((1,), (1,)), ((), ())), preferred_element_type=jnp.float32),

time: 280 us -> 281 us (level)
  Pallas kernels: 144 us -> 171 us
  blocking collectives: 31.1 us -> 19.6 us
  waiting for transfers between devices: 39.8 us -> 30.9 us
    pallas_call x0 -> x1, Pallas kernels: none -> 30.3 us  [exchange_factors(): pl.pallas_call(factor_kernel, out_shape=(jax.ShapeDtypeStruct(first.shape...]
    all_to_all x1 -> x0, waiting for transfers between devices: 18.9 us -> none  [shards(): lax.all_to_all(first.reshape(fsdp, own, rank // sub, units), 'fsdp', spli...]
    all_gather x1 -> x0, blocking collectives: 17.4 us -> none  [shards(): lax.all_gather(second, 'fsdp', axis=0, tiled=True)]
    ppermute x7, waiting for transfers between devices: 7.28 us -> 17.7 us  [swap(): return lax.ppermute(x, axis, [(0, 1), (1, 0)])]
    all_gather x1, blocking collectives: 13.7 us -> 19.6 us  [shards(): q_all = lax.all_gather(q, 'fsdp', axis=0, tiled=True)]
    all_to_all x1 -> x0, starting transfers between devices: 5.07 us -> none  [shards(): lax.all_to_all(first.reshape(fsdp, own, rank // sub, units), 'fsdp', spli...]
  transfers between devices with their start and end apart: 11 -> 10, of which waited for: 6 -> 6; matrix products, arithmetic and copies ran while one was open for 6% -> 6% of each run, Pallas kernels for 51% -> 50%
where the time goes in v4:
time: 281 us; the launch traced here: 280 us
  Pallas kernels  171 us (61%)
  waiting for transfers between devices  30.9 us (11%)
  blocking collectives  19.6 us (7%)
  between operations  14.3 us (5%)
  matrix products  12.1 us (4%)
  other arithmetic  11.8 us (4%)
  starting transfers between devices  11.6 us (4%)
  local copies, waits for them, and re-layouts  8.77 us (3%)
    pallas_call x1, Pallas kernels, base_parts(): pl.pallas_call(base_kernel, out_shape=(half, half), in_specs=[pl.BlockSpe...  141 us
    pallas_call x1, Pallas kernels, exchange_factors(): pl.pallas_call(factor_kernel, out_shape=(jax.ShapeDtypeStruct(first.shape...  30.3 us
    all_gather x1, blocking collectives, shards(): q_all = lax.all_gather(q, 'fsdp', axis=0, tiled=True)  19.6 us
    ppermute x7, waiting for transfers between devices, swap(): return lax.ppermute(x, axis, [(0, 1), (1, 0)])  17.7 us
    reduce_scatter x1, waiting for transfers between devices, shards(): grad_b = lax.psum_scatter(part_b, 'fsdp', scatter_dimension=0, tiled=True)  13.2 us
    dot_general x1, matrix products, shards(): lax.dot_general(q_wide, first, (((1,), (0,)), ((), ())), preferred_elemen...  6.84 us
    ppermute x7, starting transfers between devices, swap(): return lax.ppermute(x, axis, [(0, 1), (1, 0)])  6.34 us
    unnamed x22, local copies, waits for them, and re-layouts  5.76 us
  transfers between devices with their start and end apart: 10, of which 6 were waited for; matrix products, arithmetic and copies ran while one was open for 6% of the time, Pallas kernels for 50%

profile of v4, /device:TPU:0, one launch (start us, length us, event | category | flops | bytes accessed | tf_op | source)
XLA Modules:
  0.0 280.2 jit_solution(6253170198543720639)
XLA Ops:
  7.3 1.4 copy-done
  8.7 0.1 dynamic-slice_bitcast_fusion
  8.7 0.8 fusion.11
  9.6 1.0 dynamic-slice_bitcast_fusion.1.second_ref
  10.6 1.2 pad_maximum_fusion.2.first_ref
  11.7 30.3 %shard_map.94 = (bf16[4,32,3584]{2,1,0:T(8,128)(2,1)}, bf16[4,64,1024]{2,1,0:T(8,128)(2,1)S(1)}) custom-call(bf16[4,32,3584]{2,1,0:T(8,128)(2,1)S(1)} %pad_maximum_fusion.2.first_ref, bf16[64,1024]{1,0:T(8,128)(2,1)S(1)} %dynamic-slice_bitcast_fusion.1.second_ref), custom_call_target="tpu_custom_call" | custom-call | tf_op jit(solution)/shard_map/pallas_call | solution.py:227
  42.1 0.1 collective-permute-start.1
  42.1 0.5 collective-permute-start
  42.6 0.1 copy.18
  42.7 0.1 compare_convert_fusion
  42.8 0.1 multiply_reduce_fusion.2
  42.9 1.2 collective-permute-done.1
  44.2 1.1 broadcast_select_fusion.3
  45.3 0.1 pad_maximum_fusion.1
  45.4 0.5 fusion.9
  45.9 1.6 collective-permute-start.2
  47.4 2.4 collective-permute-done.2
  49.9 19.6 %all_gather.3 = bf16[1024,64]{0,1:T(8,128)(2,1)S(1)} all-gather(bf16[256,64]{0,1:T(8,128)(2,1)S(1)} %add_convert_fusion.2), channel_id=1, replica_groups=mesh['groups'=2,'fsdp'=4,'tp'=2,'sub'=2] {'fsdp'}, dimensions={0}, use_global_device_ids=true | all-gather | bytes 163840 | tf_op jit(solution)/shard_map/all_gather | solution.py:309
  69.5 3.2 %convolution_multiply_fusion = f32[256,3584]{1,0:T(8,128)S(1)} fusion(bf16[512,256]{0,1:T(8,128)(2,1)S(1)} %bitcast.64, bf16[1,512,3584]{2,1,0:T(8,128)(2,1)} %param.7), kind=kOutput, calls=%fused_computation.3 | convolution fusion | flops 940441600 | bytes 7602176 | tf_op jit(solution)/shard_map/dot_general | solution.py:317
  72.7 0.1 dynamic-slice_convert_fusion
  72.8 0.1 collective-permute-start.3
  72.9 1.6 broadcast_select_fusion.1
  74.5 1.0 copy-done.5
  75.5 0.3 copy-done.7
  75.8 0.1 pad_maximum_fusion
  75.9 0.2 convert_add_fusion
  76.1 1.2 copy-done.4
  77.4 1.6 collective-permute-start.4
  79.0 1.1 fusion.4
  80.1 0.7 multiply_reduce_fusion
  80.8 9.7 %collective-permute-done.4 = bf16[4,1,1,16,3584]{4,3,2,1,0:T(8,128)(2,1)} collective-permute-done((bf16[4,1,1,16,3584]{4,3,2,1,0:T(8,128)(2,1)S(1)}, bf16[4,1,1,16,3584]{4,3,2,1,0:T(8,128)(2,1)}, u32[]{:S(2)}, u32[]{:S(2)}) %collective-permute-start.4) | collective-permute-done | bytes 458784 | tf_op jit(solution)/shard_map/ppermute | solution.py:17
  90.5 2.2 fusion.6
  92.7 5.2 %all-to-all-start = ((bf16[4,16,3584]{2,1,0:T(8,128)(2,1)}), bf16[4,16,3584]{2,1,0:T(8,128)(2,1)S(1)}, u32[]{:S(2)}, u32[]{:S(2)}) async-start(bf16[4,16,3584]{2,1,0:T(8,128)(2,1)} %fusion.6), calls=%async_computation | async-start | bytes 917504 | tf_op jit(solution)/shard_map/all_to_all | solution.py:326
  97.8 140.9 %shard_map.95 = (bf16[2,256,3584]{2,1,0:T(8,128)(2,1)S(1)}, bf16[2,256,3584]{2,1,0:T(8,128)(2,1)}) custom-call(bf16[256,2048]{1,0:T(8,128)(2,1)S(1)} %bitcast.56, bf16[3584,2048]{1,0:T(8,128)(2,1)} %w_ref.1), custom_call_target="tpu_custom_call" | custom-call | flops 120259084288 | bytes 22020096 | tf_op jit(solution)/shard_map/pallas_call | solution.py:161
  238.7 1.8 copy-done.2
  240.6 0.8 copy.20
  241.4 2.5 collective-permute-start.5
  243.9 2.5 collective-permute-done.5
  246.3 0.9 broadcast_select_fusion.4
  247.2 0.4 convolution_multiply_fusion.1
  247.7 0.1 dynamic-slice_convert_fusion.1
  247.8 0.1 collective-permute-start.6
  247.9 1.9 collective-permute-done.6
  249.8 0.9 add_convert_fusion
  250.7 1.0 convert_bitcast_fusion
  251.7 6.8 %fusion.2 = bf16[1,512,3584]{2,1,0:T(8,128)(2,1)} fusion(bf16[512,3584]{1,0:T(8,128)(2,1)} %bitcast.72, bf16[512,3584]{1,0:T(8,128)(2,1)} %bitcast.57, bf16[512,4]{0,1:T(4,128)(2,1)S(1)} %get-tuple-element.37, bf16[512,64]{0,1:T(8,128)(2,1)S(1)} %constant_dynamic-slice_fusion, bf16[4,32,3584]{2,1,0:T(8,128)(2,1)} %copy-done.7, ...), kind=kOutput, calls=%fused_computation.4 | convolution fusion | flops 954335232 | bytes 12914688 | tf_op jit(solution)/shard_map/dot_general | solution.py:341
  258.5 13.2 %reduce-scatter.2.cloned.1.call-done = bf16[64,1024]{1,0:T(8,128)(2,1)} async-done(((bf16[256,1024]{1,0:T(8,128)(2,1)}), bf16[64,1024]{1,0:T(8,128)(2,1)}) %reduce-scatter.2.cloned.1.call-update) | async-done | bytes 131088 | tf_op jit(solution)/shard_map/reduce_scatter | solution.py:338
  271.8 1.6 bitcast_convert_fusion
  (34 shorter events, 0.3 us)
Async XLA Ops:
  7.2 1.5 copy-start
  7.2 35.5 %copy-start.10 = (s32[1,4,2]{1,2,0:T(2,128)S(1)}, s32[1,4,2]{1,2,0:T(2,128)}, u32[]{:S(2)}) copy-start(s32[1,4,2]{1,2,0:T(2,128)} %param.12) | copy-start | bytes 100
  7.2 35.6 %copy-start.9 = (s32[1,1024,2]{1,2,0:T(2,128)S(1)}, s32[1,1024,2]{1,2,0:T(2,128)}, u32[]{:S(2)}) copy-start(s32[1,1024,2]{1,2,0:T(2,128)} %param.13) | copy-start | bytes 24580
  7.2 234.2 %all-reduce.2.cloned.1.call-start = ((), (), s32[]{:S(2)}) async-start(), calls=%async_computation.2 | async-start | bytes 131072 | tf_op jit(solution)/shard_map/psum | solution.py:325
  9.6 35.8 %copy-start.1 = (bf16[1,256,2048]{2,1,0:T(8,128)(2,1)S(1)}, bf16[1,256,2048]{2,1,0:T(8,128)(2,1)}, u32[]{:S(2)}) copy-start(bf16[1,256,2048]{2,1,0:T(8,128)(2,1)} %param.8) | copy-start | bytes 3145732
  42.1 2.1 collective-permute-start.1
  42.1 30.8 %collective-permute-start = (bf16[4,32,3584]{2,1,0:T(8,128)(2,1)}, bf16[4,32,3584]{2,1,0:T(8,128)(2,1)}, u32[]{:S(2)}, u32[]{:S(2)}) collective-permute-start(bf16[4,32,3584]{2,1,0:T(8,128)(2,1)} %get-tuple-element.14), channel_id=1, source_target_pairs={{0,1},{1,0},{2,3},{3,2},{4,5},{5,4},{6,7},{7,6},{8,9},{9,8},{10,11... | collective-permute-start | bytes 2752520 | tf_op jit(solution)/shard_map/ppermute | solution.py:17
  45.9 4.0 %collective-permute-start.2 = (bf16[256,64]{0,1:T(8,128)(2,1)S(1)}, bf16[256,64]{0,1:T(8,128)(2,1)S(1)}, u32[]{:S(2)}, u32[]{:S(2)}) collective-permute-start(bf16[256,64]{0,1:T(8,128)(2,1)S(1)} %multiply_reduce_fusion.1), channel_id=1, source_target_pairs={{0,2},{2,0},{1,3},{3,1},{4,6},{6,4},{5,7},{7,5},{8,10},{10,8},{9,1... | collective-permute-start | bytes 98312 | tf_op jit(solution)/shard_map/ppermute | solution.py:17
  72.8 3.1 %collective-permute-start.3 = (bf16[4,2,1,16,3584]{4,3,2,1,0:T(8,128)(2,1)S(1)}, bf16[4,2,1,16,3584]{4,3,2,1,0:T(8,128)(2,1)S(1)}, u32[]{:S(2)}, u32[]{:S(2)}) collective-permute-start(bf16[4,2,1,16,3584]{4,3,2,1,0:T(8,128)(2,1)S(1)} %dynamic-slice_convert_fusion), channel_id=1, source_target_pairs={{0,1},{1,0},{2,3},{3,2},{4,5},{5,4},{6,7},{7,6},{8,9},{9,8},{10,11... | collective-permute-start | bytes 2752520 | tf_op jit(solution)/shard_map/ppermute | solution.py:17
  74.5 1.0 copy-start.5
  74.5 1.3 copy-start.7
  75.9 3.1 %copy-start.3 = (bf16[1,512,3584]{2,1,0:T(8,128)(2,1)S(1)}, bf16[1,512,3584]{2,1,0:T(8,128)(2,1)}, u32[]{:S(2)}) copy-start(bf16[1,512,3584]{2,1,0:T(8,128)(2,1)} %param.7) | copy-start | bytes 11010052
  76.1 1.2 copy-start.4
  77.4 13.1 %collective-permute-start.4 = (bf16[4,1,1,16,3584]{4,3,2,1,0:T(8,128)(2,1)S(1)}, bf16[4,1,1,16,3584]{4,3,2,1,0:T(8,128)(2,1)}, u32[]{:S(2)}, u32[]{:S(2)}) collective-permute-start(bf16[4,1,1,16,3584]{4,3,2,1,0:T(8,128)(2,1)S(1)} %dynamic-slice_convert_fusion.2), channel_id=1, source_target_pairs={{0,2},{2,0},{1,3},{3,1},{4,6},{6,4},{5,7},{7,5},{8,10},{10,8},{9,1... | collective-permute-start | bytes 1376264 | tf_op jit(solution)/shard_map/ppermute | solution.py:17
  92.7 147.9 %all-to-all-start = ((bf16[4,16,3584]{2,1,0:T(8,128)(2,1)}), bf16[4,16,3584]{2,1,0:T(8,128)(2,1)S(1)}, u32[]{:S(2)}, u32[]{:S(2)}) async-start(bf16[4,16,3584]{2,1,0:T(8,128)(2,1)} %fusion.6), calls=%async_computation | async-start | bytes 917504 | tf_op jit(solution)/shard_map/all_to_all | solution.py:326
  97.8 173.9 %reduce-scatter.2.cloned.1.call-start = ((), (), s32[]{:S(2)}) async-start(), calls=%async_computation.3 | async-start | bytes 655360 | tf_op jit(solution)/shard_map/reduce_scatter | solution.py:338
  238.7 1.8 copy-start.2
  241.4 4.9 %collective-permute-start.5 = (bf16[512,64]{0,1:T(8,128)(2,1)}, bf16[512,64]{0,1:T(8,128)(2,1)S(1)}, u32[]{:S(2)}, u32[]{:S(2)}) collective-permute-start(bf16[512,64]{0,1:T(8,128)(2,1)} %all-reduce.2.cloned.1.call-done), channel_id=1, source_target_pairs={{0,2},{2,0},{1,3},{3,1},{4,6},{6,4},{5,7},{7,5},{8,10},{10,8},{9,1... | collective-permute-start | bytes 196616 | tf_op jit(solution)/shard_map/ppermute | solution.py:17
  247.2 3.6 %copy-start.8 = (bf16[1,4,2,8,3584]{4,3,1,2,0:T(8,128)(2,1)S(1)}, bf16[1,4,2,8,3584]{4,3,1,2,0:T(8,128)(2,1)}, u32[]{:S(2)}) copy-start(bf16[1,4,2,8,3584]{4,3,1,2,0:T(8,128)(2,1)} %copy.20) | copy-start | bytes 1376260
  247.7 4.0 %copy-start.6 = (bf16[4,32,3584]{2,1,0:T(8,128)(2,1)S(1)}, bf16[4,32,3584]{2,1,0:T(8,128)(2,1)}, u32[]{:S(2)}) copy-start(bf16[4,32,3584]{2,1,0:T(8,128)(2,1)} %copy-done.5) | copy-start | bytes 2752516
  247.8 2.0 collective-permute-start.6
Sparse Core Ops, SparseCore 0:
  92.8 36.8 all-reduce.1
  250.8 20.8 reduce-scatter.1
